TPU v7x, 32 devices: a whole 2x2x4 slice. The times are simulated.
32 devices in a mesh: pt: 4 (over z), comp: 8 (over y, x, core).
Axes of the slice: x: 2, y: 2, z: 4, core: 2. Of those that a mesh axis runs over, the one named last changes fastest.
Arguments:
- spectrum: float32 [512, 131072], P(None, ('pt', 'comp')), may hold values from 0.1 to 2
- wind: float32 [131072], P(('pt', 'comp')), may hold values from 0.5 to 4
- growth: float32 [512], replicated, may hold values from 0.05 to 0.5
- whitecap: float32 [512], replicated, may hold values from 0.1 to 1
- courant: float32 [16], replicated, may hold values from 0.2 to 0.7
- substeps: int32 [512], replicated, may hold values from 1 to 8, as said below
- limiter: int32 [131072], P(('pt', 'comp')), may hold values 0 or 1
- deck: int32 [131072], replicated, may hold values from 0 to 131071, as said below
- wet: int32 [256, 512], replicated, may hold values 0 or 1
Outputs:
- spectrum_out: float32 [512, 131072], P(None, ('pt', 'comp'))
- height: float32 [131072], P(('pt', 'comp'))
Inputs may be any that keep to these rules, and one draw needn't show every extreme that they name: Every component has 1 to 8 substeps, and some component has exactly 8. Each grid cell appears at exactly one deck slot. The deck is dealt in aligned runs of 128 slots: slots k * 128 .. k * 128 + 127 hold 128 consecutive cells, in order, starting at a multiple of 128.
All inputs are finite; a program needn't handle non-finite values. No bound on the sum of `limiter` on one device may be relied on, other than what follows from the above.
Results may differ from a plain program's by a relative error of at most 0.0003.
Values sent between devices are 32-bit elements; how exact they have to be, the bound alone decides.
No kernel may reach another device: no remote copies, remote signals or barrier semaphores. Data moves between devices by JAX's collectives and lax.ppermute only.
A program may use at most 128 MiB of HBM per device.

v0:
```python
import math

import jax
import jax.numpy as jnp
from jax import lax
from jax.sharding import PartitionSpec as P

DIRS = 32
MAXSUB = 8
RUN = 128


rate_limit = 0.5
time_step = 0.5


def sources(spectrum, wind, growth, whitecap, limiter):
    mean_energy = jnp.mean(spectrum, axis=0)
    rate = (
        wind[None, :] * growth[:, None]
        - whitecap[:, None] * (mean_energy / (1.0 + mean_energy))[None, :]
    )
    rate = jnp.where(limiter[None, :] == 1, rate_limit * jnp.tanh(rate / rate_limit), rate)
    return spectrum * jnp.exp(time_step * rate)


def substep(field_grid, cross, along, wetness):
    sea = field_grid * wetness[None, :, :]
    east = jnp.roll(sea, 1, axis=2)
    west = jnp.roll(sea, -1, axis=2)
    up_column = jnp.where(along[:, None, None] > 0, east, west)
    zero_row = jnp.zeros_like(sea[:, :1, :])
    south = jnp.concatenate([zero_row, sea[:, :-1, :]], axis=1)
    north = jnp.concatenate([sea[:, 1:, :], zero_row], axis=1)
    up_row = jnp.where(cross[:, None, None] > 0, south, north)
    moved = (
        field_grid
        - jnp.abs(cross)[:, None, None] * (field_grid - up_row)
        - jnp.abs(along)[:, None, None] * (field_grid - up_column)
    )
    return jnp.where(wetness[None, :, :] > 0, moved, field_grid)


def on_device(spectrum, wind, growth, whitecap, courant, substeps, limiter, deck, wet):
    forced = sources(spectrum, wind, growth, whitecap, limiter)
    pt_count = lax.axis_size("pt")
    comp_count = lax.axis_size("comp")
    group_size = pt_count * comp_count
    total_comps = forced.shape[0]
    point_count = forced.shape[1]
    per_device = total_comps // group_size
    all_points = deck.shape[0]
    rows_grid = wet.shape[0]
    cols_grid = wet.shape[1]
    run_count = all_points // RUN
    positions = jnp.arange(total_comps, dtype=jnp.int32)
    received = lax.all_to_all(
        forced.reshape(per_device, group_size, point_count),
        ("pt", "comp"),
        split_axis=1,
        concat_axis=1,
        tiled=True,
    )
    fields = received.reshape(per_device, run_count, RUN)
    own_rank = lax.axis_index("pt") * comp_count + lax.axis_index("comp")
    comps = positions[jnp.arange(per_device, dtype=jnp.int32) * group_size + own_rank]
    angle = 2.0 * math.pi / DIRS * ((comps % DIRS).astype(jnp.float32) + 0.5)
    speed = courant[comps // DIRS]
    cross = speed * jnp.sin(angle)
    along = speed * jnp.cos(angle)
    counts = substeps[comps]
    wetness = wet.astype(jnp.float32)
    slot_runs = deck.reshape(run_count, RUN)[:, 0] // RUN
    run_ids = jnp.arange(run_count, dtype=jnp.int32)
    matches = slot_runs[None, :] == run_ids[:, None]
    cell_runs = jnp.sum(jnp.where(matches, run_ids[None, :], 0), axis=1)
    field_grid = jnp.take(fields, cell_runs, axis=1).reshape(per_device, rows_grid, cols_grid)
    for step in range(MAXSUB):
        field_grid = jnp.where(
            step < counts[:, None, None], substep(field_grid, cross, along, wetness), field_grid
        )
    slots = jnp.take(field_grid.reshape(per_device, run_count, RUN), slot_runs, axis=1).reshape(
        per_device, all_points
    )
    back = lax.all_to_all(
        slots.reshape(per_device, group_size, point_count),
        ("pt", "comp"),
        split_axis=1,
        concat_axis=1,
        tiled=True,
    )
    arrived = back.reshape(total_comps, point_count)
    height = 4.0 * jnp.sqrt(jnp.mean(arrived, axis=0) + 1e-06)
    return (arrived, height)


def solution(mesh):
    in_specs = (
        P(None, ("pt", "comp")),
        P(("pt", "comp")),
        P(),
        P(),
        P(),
        P(),
        P(("pt", "comp")),
        P(),
        P(),
    )
    out_specs = (P(None, ("pt", "comp")), P(("pt", "comp")))
    return jax.shard_map(
        on_device, mesh=mesh, in_specs=in_specs, out_specs=out_specs, check_vma=False
    )
```

profile of v0, /device:TPU:0, one launch (start us, length us, event | category | flops | bytes accessed | tf_op | source)
XLA Modules:
  0.0 793.8 jit_solution(5377908040328651239)
XLA Ops:
  10.8 8.3 %copy.29 = f32[16,32,4096]{2,0,1:T(8,128)} copy(f32[16,32,4096]{2,1,0:T(8,128)S(1)} %bitcast.32) | data formatting | bytes 16777216 | tf_op jit(solution)/shard_map/reshape | solution.py:58
  19.0 7.9 all-to-all-start
  32.5 180.5 %all-to-all-done = f32[16,32,4096]{2,0,1:T(8,128)} async-done(((f32[16,32,4096]{2,0,1:T(8,128)}), f32[16,32,4096]{2,0,1:T(8,128)}, u32[]{:S(2)}, u32[]{:S(2)}) %all-to-all-start) | async-done | bytes 8388640 | tf_op jit(solution)/shard_map/all_to_all | solution.py:57
  213.0 11.6 %copy.30 = f32[16,32,4096]{2,1,0:T(8,128)} copy(f32[16,32,4096]{2,0,1:T(8,128)} %all-to-all-done) | data formatting | bytes 16777216 | tf_op jit(solution)/shard_map/all_to_all | solution.py:57
  224.6 9.3 %reshape.228 = f32[16,1024,128]{2,1,0:T(8,128)} reshape(f32[16,32,4096]{2,1,0:T(8,128)} %copy.30) | data formatting | bytes 16777216 | tf_op jit(solution)/shard_map/reshape | solution.py:64
  233.9 11.6 %copy.31 = f32[16,1024,128]{2,0,1:T(8,128)} copy(f32[16,1024,128]{2,1,0:T(8,128)} %reshape.228) | data formatting | bytes 16777216 | tf_op jit(solution)/shard_map/reshape | solution.py:64
  245.5 13.1 %gather_fusion.3 = f32[1024,16,128]{2,1,0:T(8,128)} fusion(f32[16,1024,128]{2,0,1:T(8,128)} %copy.31, s32[1024]{0:T(1024)S(1)} %fusion.26), kind=kCustom, calls=%fused_computation.clone | custom fusion | bytes 16781312 | tf_op jit(solution)/shard_map/jit(_take)/gather | solution.py:77
  258.6 6.9 select_bitcast_fusion.1
  271.5 9.4 %reshape.230 = f32[16,256,512]{2,1,0:T(8,128)} reshape(f32[16,1024,128]{2,1,0:T(8,128)} %copy.32) | data formatting | bytes 16777216 | tf_op jit(solution)/shard_map/reshape | solution.py:77
  286.2 7.4 fusion.61
  300.3 15.4 %broadcast_multiply_fusion.6 = (f32[16,256,512]{2,1,0:T(8,128)S(1)}, f32[16,256,512]{2,1,0:T(8,128)}) fusion(f32[256,512]{1,0:T(8,128)} %copy-done.3, f32[16,256,512]{2,1,0:T(8,128)S(1)} %bitcast.25, f32[16,256,1]{2,1,0:T(8,128)S(1)} %get-tuple-element.66, f32[16,256,511]{2,1,0:T(8,128)} %get-tuple-element.68, f32[16,256,511]{2,1,0:T(8,128)} %get-tuple-element.67, ...), kind=kLoop, calls=%fused_computation.54 | loop fusion | flops 27262976 | bytes 59310256 | tf_op jit(solution)/shard_map/mul | solution.py:28
  316.5 7.4 fusion.58
  330.8 14.9 %broadcast_multiply_fusion.5 = (f32[16,256,512]{2,1,0:T(8,128)S(1)}, f32[16,256,512]{2,1,0:T(8,128)S(1)}) fusion(f32[256,512]{1,0:T(8,128)} %copy-done.3, f32[16,256,512]{2,1,0:T(8,128)} %get-tuple-element.18, f32[16,256,1]{2,1,0:T(8,128)S(1)} %get-tuple-element.60, f32[16,256,511]{2,1,0:T(8,128)} %get-tuple-element.62, ...), kind=kLoop, calls=%fused_computation.53 | loop fusion | flops 27262976 | bytes 59310256 | tf_op jit(solution)/shard_map/mul | solution.py:28
  346.6 7.4 fusion.55
  360.6 15.4 %broadcast_multiply_fusion.4 = (f32[16,256,512]{2,1,0:T(8,128)S(1)}, f32[16,256,512]{2,1,0:T(8,128)}) fusion(f32[256,512]{1,0:T(8,128)} %copy-done.3, f32[16,256,512]{2,1,0:T(8,128)S(1)} %get-tuple-element.16, f32[16,256,1]{2,1,0:T(8,128)S(1)} %get-tuple-element.54, f32[16,256,511]{2,1,0:T(8,128)} %get-tuple-element.56, ...), kind=kLoop, calls=%fused_computation.52 | loop fusion | flops 27262976 | bytes 59310256 | tf_op jit(solution)/shard_map/mul | solution.py:28
  376.8 7.4 fusion.52
  390.9 15.8 %broadcast_multiply_fusion.3 = (f32[16,256,512]{2,1,0:T(8,128)S(1)}, f32[16,256,512]{2,1,0:T(8,128)}) fusion(f32[256,512]{1,0:T(8,128)} %copy-done.3, f32[16,256,512]{2,1,0:T(8,128)S(1)} %bitcast.27, f32[16,256,1]{2,1,0:T(8,128)S(1)} %get-tuple-element.48, f32[16,256,511]{2,1,0:T(8,128)} %get-tuple-element.50, f32[16,256,511]{2,1,0:T(8,128)} %get-tuple-element.49, ...), kind=kLoop, calls=%fused_computation.51 | loop fusion | flops 27262976 | bytes 59310256 | tf_op jit(solution)/shard_map/mul | solution.py:28
  407.6 7.4 fusion.49
  421.7 15.4 %broadcast_multiply_fusion.2 = (f32[16,256,512]{2,1,0:T(8,128)S(1)}, f32[16,256,512]{2,1,0:T(8,128)}) fusion(f32[256,512]{1,0:T(8,128)} %copy-done.3, f32[16,256,512]{2,1,0:T(8,128)S(1)} %bitcast.29, f32[16,256,1]{2,1,0:T(8,128)S(1)} %get-tuple-element.42, f32[16,256,511]{2,1,0:T(8,128)} %get-tuple-element.44, f32[16,256,511]{2,1,0:T(8,128)} %get-tuple-element.43, ...), kind=kLoop, calls=%fused_computation.50 | loop fusion | flops 27262976 | bytes 59310256 | tf_op jit(solution)/shard_map/mul | solution.py:28
  437.9 7.4 fusion.46
  451.9 15.0 %broadcast_multiply_fusion.1 = (f32[16,256,512]{2,1,0:T(8,128)S(1)}, f32[16,256,512]{2,1,0:T(8,128)S(1)}) fusion(f32[256,512]{1,0:T(8,128)} %copy-done.3, f32[16,256,512]{2,1,0:T(8,128)} %get-tuple-element.10, f32[16,256,1]{2,1,0:T(8,128)S(1)} %get-tuple-element.36, f32[16,256,511]{2,1,0:T(8,128)} %get-tuple-element.38, ...), kind=kLoop, calls=%fused_computation.49 | loop fusion | flops 27262976 | bytes 59310256 | tf_op jit(solution)/shard_map/mul | solution.py:28
  467.7 7.4 fusion.43
  482.0 15.4 %broadcast_multiply_fusion = (f32[16,256,512]{2,1,0:T(8,128)S(1)}, f32[16,256,512]{2,1,0:T(8,128)}) fusion(f32[256,512]{1,0:T(8,128)} %copy-done.3, f32[16,256,512]{2,1,0:T(8,128)S(1)} %get-tuple-element.8, f32[16,256,1]{2,1,0:T(8,128)S(1)} %get-tuple-element.30, f32[16,256,511]{2,1,0:T(8,128)} %get-tuple-element.32, f32[16,256,511]{2,1,0:T(8,128)} %get-tuple-element.31, ...), kind=kLoop, calls=%fused_computation.48 | loop fusion | flops 27262976 | bytes 59310256 | tf_op jit(solution)/shard_map/mul | solution.py:28
  498.2 7.3 fusion.39
  512.2 15.1 %select_select_fusion = f32[16,256,512]{2,1,0:T(8,128)} fusion(f32[16,256,512]{2,1,0:T(8,128)S(1)} %bitcast.31, f32[16,256,511]{2,1,0:T(8,128)} %get-tuple-element.24, f32[16,256,1]{2,1,0:T(8,128)S(1)} %get-tuple-element.26, f32[16,256,1]{2,1,0:T(8,128)S(1)} %get-tuple-element.25, f32[16,256,511]{2,1,0:T(8,128)} %get-tuple-element.23, ...), kind=kLoop, calls=%fused_computation.5 | loop fusion | flops 25165824 | bytes 50397360 | tf_op jit(solution)/shard_map/jit(_where)/select_n | solution.py:79
  527.3 9.1 %reshape.231 = f32[16,1024,128]{2,1,0:T(8,128)} reshape(f32[16,256,512]{2,1,0:T(8,128)} %select_select_fusion) | data formatting | bytes 16777216 | tf_op jit(solution)/shard_map/reshape | solution.py:82
  536.4 11.6 %copy.33 = f32[16,1024,128]{2,0,1:T(8,128)} copy(f32[16,1024,128]{2,1,0:T(8,128)} %reshape.231) | data formatting | bytes 16777216 | tf_op jit(solution)/shard_map/reshape | solution.py:82
  548.0 12.9 %gather_fusion.4 = f32[1024,16,128]{2,1,0:T(8,128)} fusion(f32[16,1024,128]{2,0,1:T(8,128)} %copy.33, s32[1024]{0:T(1024)S(1)} %copy-done.7), kind=kCustom, calls=%fused_computation.1.clone | custom fusion | bytes 16781312 | tf_op jit(solution)/shard_map/jit(_take)/gather | solution.py:82
  573.6 9.7 %reshape_reshape.3 = f32[16,32,4096]{2,1,0:T(8,128)} reshape(f32[16,1024,128]{2,1,0:T(8,128)} %copy.34) | data formatting | bytes 16777216 | tf_op jit(solution)/shard_map/reshape;reshape | solution.py:86
  583.2 8.2 %copy.35 = f32[16,32,4096]{2,0,1:T(8,128)S(1)} copy(f32[16,32,4096]{2,1,0:T(8,128)} %reshape_reshape.3) | data formatting | bytes 16777216 | tf_op jit(solution)/shard_map/reshape;reshape | solution.py:86
  591.5 186.0 %all_to_all.10 = f32[16,32,4096]{2,0,1:T(8,128)} all-to-all(f32[16,32,4096]{2,0,1:T(8,128)S(1)} %copy.35), channel_id=1, replica_groups=mesh['pt'=4,'comp'=8] {'pt','comp'}, dimensions={1} | all-to-all | bytes 16777216 | tf_op jit(solution)/shard_map/all_to_all | solution.py:85
  781.9 11.6 %copy.36 = f32[16,32,4096]{2,1,0:T(8,128)} copy(f32[16,32,4096]{2,0,1:T(8,128)} %all_to_all.10) | data formatting | bytes 16777216 | tf_op jit(solution)/shard_map/all_to_all | solution.py:85
  (100 shorter events, 103.2 us)
Async XLA Ops:
  0.6 27.8 %copy-start = (s32[512]{0:T(512)S(1)}, s32[512]{0:T(512)}, u32[]{:S(2)}) copy-start(s32[512]{0:T(512)} %param.16) | copy-start | bytes 6148
  0.6 4.6 copy-start.11
  0.7 4.6 copy-start.12
  0.7 4.6 copy-start.8
  19.0 7.9 copy-start.5
  19.0 8.7 %copy-start.2 = (f32[16]{0:T(128)S(1)}, f32[16]{0:T(128)}, u32[]{:S(2)}) copy-start(f32[16]{0:T(128)} %param.15) | copy-start | bytes 196
  19.0 10.1 %copy-start.6 = (s32[131072]{0:T(1024)S(1)}, s32[131072]{0:T(1024)}, u32[]{:S(2)}) copy-start(s32[131072]{0:T(1024)} %param.18) | copy-start | bytes 1572868
  19.0 193.9 %all-to-all-start = ((f32[16,32,4096]{2,0,1:T(8,128)}), f32[16,32,4096]{2,0,1:T(8,128)}, u32[]{:S(2)}, u32[]{:S(2)}) async-start(f32[16,32,4096]{2,0,1:T(8,128)} %copy.29), calls=%async_computation | async-start | bytes 16777216 | tf_op jit(solution)/shard_map/all_to_all | solution.py:57
  27.0 253.9 %copy-start.3 = (f32[256,512]{1,0:T(8,128)}, f32[256,512]{1,0:T(8,128)S(1)}, u32[]{:S(2)}) copy-start(f32[256,512]{1,0:T(8,128)S(1)} %convert_element_type.19) | copy-start | bytes 1572868
  286.2 14.1 %slice-start = ((s8[8388608]{0:T(1024)(128)(4,1)}), s8[4194304]{0:T(1024)(128)(4,1)S(1)}, s32[]{:S(2)}) async-start(s8[8388608]{0:T(1024)(128)(4,1)} %bitcast.24), calls=%async_computation.2 | async-start | bytes 8388608
  293.7 6.7 slice-start.1
  376.8 14.1 %slice-start.2 = ((s8[8388608]{0:T(1024)(128)(4,1)}), s8[4194304]{0:T(1024)(128)(4,1)S(1)}, s32[]{:S(2)}) async-start(s8[8388608]{0:T(1024)(128)(4,1)} %bitcast.26), calls=%async_computation.4 | async-start | bytes 8388608
  384.2 6.7 slice-start.3
  384.3 6.7 copy-start.16
  407.5 14.1 %slice-start.4 = ((s8[8388608]{0:T(1024)(128)(4,1)}), s8[4194304]{0:T(1024)(128)(4,1)S(1)}, s32[]{:S(2)}) async-start(s8[8388608]{0:T(1024)(128)(4,1)} %bitcast.28), calls=%async_computation.6 | async-start | bytes 8388608
  415.0 6.7 slice-start.5
  415.0 6.7 copy-start.15
  445.3 6.7 copy-start.14
  475.1 6.8 copy-start.13
  498.2 14.0 %slice-start.6 = ((s8[8388608]{0:T(1024)(128)(4,1)}), s8[4194304]{0:T(1024)(128)(4,1)S(1)}, s32[]{:S(2)}) async-start(s8[8388608]{0:T(1024)(128)(4,1)} %bitcast.30), calls=%async_computation.8 | async-start | bytes 8388608
  505.5 6.7 slice-start.7
  505.5 6.7 copy-start.4
  505.5 6.7 copy-start.10
  536.4 11.6 %copy-start.7 = (s32[1024]{0:T(1024)S(1)}, s32[1024]{0:T(1024)}, u32[]{:S(2)}) copy-start(s32[1024]{0:T(1024)} %fusion.27) | copy-start | bytes 12292
  548.0 12.9 %copy-start.9 = (pred[1024]{0:T(1024)(128)(4,1)S(1)}, pred[1024]{0:T(1024)(128)(4,1)}, u32[]{:S(2)}) copy-start(pred[1024]{0:T(1024)(128)(4,1)} %get-tuple-element.3) | copy-start | bytes 3076
  781.3 12.3 %copy-start.1 = (s32[512]{0:T(512)S(1)}, s32[512]{0:T(512)}, u32[]{:S(2)}) copy-start(s32[512]{0:T(512)} %param.16) | copy-start | bytes 6148
where the time goes:
time: 801 us; the launch traced here: 794 us
  local copies, waits for them, and re-layouts  260 us (32%)
  blocking collectives  186 us (23%)
  waiting for transfers between devices  180 us (22%)
  other arithmetic  158 us (20%)
    all_to_all x1, blocking collectives, on_device(): lax.all_to_all(slots.reshape(per_device, group_size, point_count), ('pt',...  186 us
    all_to_all x1, waiting for transfers between devices, on_device(): lax.all_to_all(forced.reshape(per_device, group_size, point_count), ('pt'...  180 us
    mul x8, other arithmetic, substep(): sea = field_grid * wetness[None, :, :]  112 us
    slice x14, local copies, waits for them, and re-layouts, substep(): east = jnp.roll(sea, 1, axis=2)  57.5 us
    slice x8, local copies, waits for them, and re-layouts, substep(): south = jnp.concatenate([zero_row, sea[:, :-1, :]], axis=1)  53.6 us
    reshape x2, local copies, waits for them, and re-layouts, on_device(): fields = received.reshape(per_device, run_count, RUN)  20.9 us
    reshape x2, local copies, waits for them, and re-layouts, on_device(): field_grid.reshape(per_device, run_count, RUN)  20.7 us
    another operation x2, local copies, waits for them, and re-layouts, on_device(): slots.reshape(per_device, group_size, point_count)  17.9 us
  transfers between devices with their start and end apart: 1, of which 1 were waited for; matrix products, arithmetic and copies ran while one was open for 1% of the time, Pallas kernels for 0%

commit v1 on v0

v1 whole, which is shorter than its diff:
```python
import math

import jax
import jax.numpy as jnp
from jax import lax
from jax.experimental import pallas as pl
from jax.experimental.pallas import tpu as pltpu
from jax.sharding import PartitionSpec as P

DIRS = 32
MAXSUB = 8
RUN = 128
SUB = 8

rate_limit = 0.5
time_step = 0.5

MIB = 1024 * 1024


def plain_sources(spectrum, wind, growth, whitecap, limiter):
    mean_energy = jnp.mean(spectrum, axis=0)
    rate = (
        wind[None, :] * growth[:, None]
        - whitecap[:, None] * (mean_energy / (1.0 + mean_energy))[None, :]
    )
    rate = jnp.where(limiter[None, :] == 1, rate_limit * jnp.tanh(rate / rate_limit), rate)
    return spectrum * jnp.exp(time_step * rate)


def plain_substep(field_grid, cross, along, wetness):
    sea = field_grid * wetness[None, :, :]
    east = jnp.roll(sea, 1, axis=2)
    west = jnp.roll(sea, -1, axis=2)
    up_column = jnp.where(along[:, None, None] > 0, east, west)
    zero_row = jnp.zeros_like(sea[:, :1, :])
    south = jnp.concatenate([zero_row, sea[:, :-1, :]], axis=1)
    north = jnp.concatenate([sea[:, 1:, :], zero_row], axis=1)
    up_row = jnp.where(cross[:, None, None] > 0, south, north)
    moved = (
        field_grid
        - jnp.abs(cross)[:, None, None] * (field_grid - up_row)
        - jnp.abs(along)[:, None, None] * (field_grid - up_column)
    )
    return jnp.where(wetness[None, :, :] > 0, moved, field_grid)


def plain(spectrum, wind, growth, whitecap, courant, substeps, limiter, deck, wet):
    forced = plain_sources(spectrum, wind, growth, whitecap, limiter)
    comp_count = lax.axis_size("comp")
    group_size = lax.axis_size("pt") * comp_count
    total_comps, point_count = forced.shape
    per_device = total_comps // group_size
    all_points = deck.shape[0]
    rows_grid, cols_grid = wet.shape
    run_count = all_points // RUN
    received = lax.all_to_all(
        forced.reshape(per_device, group_size, point_count),
        ("pt", "comp"),
        split_axis=1,
        concat_axis=1,
        tiled=True,
    )
    fields = received.reshape(per_device, run_count, RUN)
    own_rank = lax.axis_index("pt") * comp_count + lax.axis_index("comp")
    comps = jnp.arange(per_device, dtype=jnp.int32) * group_size + own_rank
    cross, along = courants(comps, courant)
    counts = substeps[comps]
    wetness = wet.astype(jnp.float32)
    slot_runs = deck.reshape(run_count, RUN)[:, 0] // RUN
    cell_runs = jnp.zeros((run_count,), jnp.int32).at[slot_runs].set(
        jnp.arange(run_count, dtype=jnp.int32)
    )
    field_grid = jnp.take(fields, cell_runs, axis=1).reshape(per_device, rows_grid, cols_grid)
    for step in range(MAXSUB):
        field_grid = jnp.where(
            step < counts[:, None, None],
            plain_substep(field_grid, cross, along, wetness),
            field_grid,
        )
    slots = jnp.take(field_grid.reshape(per_device, run_count, RUN), slot_runs, axis=1)
    back = lax.all_to_all(
        slots.reshape(per_device, group_size, point_count),
        ("pt", "comp"),
        split_axis=1,
        concat_axis=1,
        tiled=True,
    )
    arrived = back.reshape(total_comps, point_count)
    height = 4.0 * jnp.sqrt(jnp.mean(arrived, axis=0) + 1e-06)
    return (arrived, height)


def courants(comps, courant):
    angle = 2.0 * math.pi / DIRS * ((comps % DIRS).astype(jnp.float32) + 0.5)
    speed = courant[comps // DIRS]
    return speed * jnp.sin(angle), speed * jnp.cos(angle)


def lane_gather(x, idx):
    dims = lax.GatherDimensionNumbers(
        offset_dims=(),
        collapsed_slice_dims=(1,),
        start_index_map=(1,),
        operand_batching_dims=(0,),
        start_indices_batching_dims=(0,),
    )
    return lax.gather(
        x, idx[..., None], dims, slice_sizes=(1, 1), mode=lax.GatherScatterMode.PROMISE_IN_BOUNDS
    )


def lanes(rows=SUB):
    return lax.broadcasted_iota(jnp.int32, (rows, RUN), 1)


def rows_of(block, j):
    return jnp.broadcast_to(block[j : j + 1, :], (SUB, RUN))


def place(off, cap):
    first = jnp.minimum(off // RUN, cap - 1)
    return first, off - first * RUN


def columns(t):
    return slice(t * RUN, (t + 1) * RUN)


def write_stream(values, spots, lane, store, cap):
    merged = values[0]
    for t, (value, (first, start)) in enumerate(zip(values, spots)):
        if t > 0:
            before = jnp.where(first == spots[t - 1][0], merged, values[t - 1])
            merged = jnp.where(lane >= start, value, before)
        if t == len(values) - 1:
            store(jnp.minimum(first + 1, cap - 1), value)
        store(first, merged)


def force(value, wind, ratio, limited, growth, whitecap):
    rate = wind * growth - whitecap * ratio
    rate = jnp.where(limited, rate_limit * jnp.tanh(rate / rate_limit), rate)
    return value * jnp.exp(time_step * rate)


def spread(row):
    return jnp.transpose(jnp.broadcast_to(row, (RUN, RUN)))


def begin_kernel(
    small, runs, row_runs, rank, deck, wet, wind, limiter, growth, whitecap, spectrum,
    held, sent_small, sent_full, idxu, idxp, offs, own_idxu, own_idxp, own_off, ratio, need,
    values, packed, sea, total, grown, capped, off, in_sems, held_sems, sent_sems, off_sem,
):
    comps = values.shape[0]
    slots = deck.shape[0]
    groups = packed.shape[0] // runs
    parts = in_sems.shape[0]
    part = comps // parts

    def fetch(p):
        rows = pl.ds(p * part, part)
        return pltpu.make_async_copy(spectrum.at[rows], values.at[rows], in_sems.at[p])

    for p in range(parts):
        fetch(p).start()

    halves = wet.shape[0] // RUN
    for q in range(row_runs):
        for h in range(halves):
            k = q * halves + h
            sea[k * RUN : (k + 1) * RUN, :] = wet[h * RUN : (h + 1) * RUN, columns(q)].astype(
                jnp.float32
            ).astype(jnp.bfloat16)

    lane = lanes(RUN)
    row = lax.broadcasted_iota(jnp.int32, (RUN, RUN), 0)
    one = lambda mask: jnp.where(mask, 1.0, 0.0).astype(jnp.bfloat16)
    earlier = one(row < lane)
    ones = jnp.ones((RUN, RUN), jnp.bfloat16)
    runs_before = one((lane < row) & (lane // runs == row // runs))
    dot = lambda a, b: jnp.dot(a, b, preferred_element_type=jnp.float32)

    def tables(b, most):
        here = pl.ds(pl.multiple_of(b * RUN, RUN), RUN)
        slot = deck[here, :] // RUN
        picks = [
            one(slot == lane * row_runs + (h * RUN * row_runs + q))
            for q in range(row_runs)
            for h in range(halves)
        ]
        wet_here = dot(jnp.concatenate(picks, axis=1), sea[...])
        wet_low = wet_here.astype(jnp.bfloat16)
        prefix = dot(wet_low, earlier)
        count = dot(wet_low, ones)
        off_f = dot(runs_before, count.astype(jnp.bfloat16))
        off_i = off_f.astype(jnp.int32)
        through = (prefix + wet_here).astype(jnp.int32)
        spot = jnp.bitwise_and(off_i + prefix.astype(jnp.int32), RUN - 1)
        idxu[here, :] = jnp.where(wet_here > 0.5, spot, spot + RUN)
        offs[here, :] = off_i
        nth = jnp.bitwise_and(lane - off_i, RUN - 1)
        at = jnp.zeros((RUN, RUN), jnp.int32)
        bit = RUN // 2
        while bit:
            probe = lane_gather(through, at + (bit - 1))
            at = jnp.where(probe <= nth, at + bit, at)
            bit //= 2
        idxp[here, :] = at
        return jnp.maximum(most, jnp.max(off_f + count))

    most = lax.fori_loop(0, slots // RUN, tables, jnp.float32(0)).astype(jnp.int32)
    need[0] = most
    mine = pl.ds(pl.multiple_of(rank[0] * runs, SUB), runs)
    own_idxu[...] = idxu[mine, :]
    own_idxp[...] = idxp[mine, :]
    own_off[...] = offs[mine, :]
    off_copy = pltpu.make_async_copy(own_off, off, off_sem)
    off_copy.start()

    for r in range(grown.shape[0] // RUN):
        rows = slice(r * RUN, (r + 1) * RUN)
        grown[rows, :] = spread(growth[r : r + 1, :])
        capped[rows, :] = spread(whitecap[r : r + 1, :])

    for p in range(parts):
        fetch(p).wait()
        for t in range(runs):
            cols = columns(t)
            added = [values[p * part + g * SUB : p * part + (g + 1) * SUB, cols] for g in range(part // SUB)]
            while len(added) > 1:
                added = [sum(added[k : k + 2]) for k in range(0, len(added), 2)]
            total[:, cols] = added[0] if p == 0 else total[:, cols] + added[0]
    mean = jnp.sum(total[...], axis=0, keepdims=True) / comps
    ratio[...] = jnp.broadcast_to(mean / (1.0 + mean), ratio.shape)

    off_copy.wait()
    cap = jnp.where(most <= small * RUN, small, runs)
    reg_lane = lanes()

    def keep(g):
        rows = pl.ds(pl.multiple_of(g * SUB, SUB), SUB)
        return pltpu.make_async_copy(values.at[rows], held.at[rows], held_sems.at[g])

    def pass_on(g, size, target):
        regs = pl.ds(g * size, size)
        return pltpu.make_async_copy(packed.at[regs], target.at[regs], sent_sems.at[g])

    def group(g, carry):
        rows = pl.ds(pl.multiple_of(g * SUB, SUB), SUB)
        growth_g = grown[rows, :]
        whitecap_g = capped[rows, :]
        forced = []
        for t in range(runs):
            cols = columns(t)
            wind_t = jnp.broadcast_to(wind[:, cols], (SUB, RUN))
            limited = jnp.broadcast_to(limiter[:, cols], (SUB, RUN)) == 1
            forced.append(force(values[rows, cols], wind_t, ratio[:, cols], limited, growth_g, whitecap_g))
        for t in range(runs):
            values[rows, columns(t)] = forced[t]
        keep(g).start()
        sent = [lane_gather(forced[t], rows_of(own_idxp, t)) for t in range(runs)]
        spots = [place(off[t, 0], cap) for t in range(runs)]

        def store(at, value):
            packed[g * cap + at] = value

        write_stream(sent, spots, reg_lane, store, cap)

        @pl.when(most <= small * RUN)
        def _():
            pass_on(g, small, sent_small).start()

        @pl.when(most > small * RUN)
        def _():
            pass_on(g, runs, sent_full).start()

        return carry

    lax.fori_loop(0, groups, group, 0)

    def drain(g, carry):
        keep(g).wait()

        @pl.when(most <= small * RUN)
        def _():
            pass_on(g, small, sent_small).wait()

        @pl.when(most > small * RUN)
        def _():
            pass_on(g, runs, sent_full).wait()

        return carry

    lax.fori_loop(0, groups, drain, 0)


def begin(small, runs, row_runs, groups, rank, deck, wet, wind, limiter, growth, whitecap, spectrum):
    comps, points = spectrum.shape
    slots = deck.shape[0]
    block = groups * SUB
    parts = 8
    smem = pl.BlockSpec(memory_space=pltpu.SMEM)
    vmem = pl.BlockSpec(memory_space=pltpu.VMEM)
    far = pl.BlockSpec(memory_space=pl.ANY)
    cells = comps * points
    f32 = lambda *shape: jax.ShapeDtypeStruct(shape, jnp.float32)
    i32 = lambda *shape: jax.ShapeDtypeStruct(shape, jnp.int32)

    def body(*refs):
        begin_kernel(small, runs, row_runs, *refs)

    return pl.pallas_call(
        body,
        in_specs=[smem, vmem, vmem, vmem, vmem, vmem, vmem, far],
        out_specs=[far] * 3 + [vmem] * 7 + [smem],
        out_shape=[
            f32(block, points),
            f32(groups * small, SUB, RUN),
            f32(groups * runs, SUB, RUN),
            i32(slots, RUN),
            i32(slots, RUN),
            i32(slots, RUN),
            i32(runs, RUN),
            i32(runs, RUN),
            i32(runs, RUN),
            f32(SUB, points),
            i32(1),
        ],
        scratch_shapes=[
            pltpu.VMEM((comps, points), jnp.float32),
            pltpu.VMEM((groups * runs, SUB, RUN), jnp.float32),
            pltpu.VMEM((slots, RUN), jnp.bfloat16),
            pltpu.VMEM((SUB, points), jnp.float32),
            pltpu.VMEM((block, RUN), jnp.float32),
            pltpu.VMEM((block, RUN), jnp.float32),
            pltpu.SMEM((runs, RUN), jnp.int32),
            pltpu.SemaphoreType.DMA((parts,)),
            pltpu.SemaphoreType.DMA((groups,)),
            pltpu.SemaphoreType.DMA((groups,)),
            pltpu.SemaphoreType.DMA,
        ],
        cost_estimate=pl.CostEstimate(flops=10 * cells, bytes_accessed=10 * cells, transcendentals=cells),
        compiler_params=pltpu.CompilerParams(vmem_limit_bytes=32 * MIB),
        name="begin",
    )(rank, deck, wet, wind, limiter, growth, whitecap, spectrum)


def source_kernel(cap, runs, off, wind, limiter, ratio, growth, whitecap, idxp, spectrum, forced, packed):
    groups = spectrum.shape[0] // SUB
    lane = lanes()
    block = groups * SUB
    step = pl.program_id(0)
    grown = spread(growth[...].reshape(1, RUN))
    capped = spread(whitecap[...].reshape(1, RUN))
    spots = [place(off[t, 0], cap) for t in range(runs)]
    for g in range(groups):
        rows = slice(g * SUB, (g + 1) * SUB)
        values = []
        for t in range(runs):
            cols = columns(t)
            wind_t = jnp.broadcast_to(wind[:, cols], (SUB, RUN))
            limited = jnp.broadcast_to(limiter[:, cols], (SUB, RUN)) == 1
            values.append(
                force(spectrum[rows, cols], wind_t, ratio[:, cols], limited, grown[rows, :], capped[rows, :])
            )
        for t in range(runs):
            forced[rows, columns(t)] = values[t]
        sent = [lane_gather(values[t], rows_of(idxp, t)) for t in range(runs)]

        def store(at, value, g=g):
            packed[g, at] = value

        write_stream(sent, spots, lane, store, cap)


def sources(cap, chunk, groups, off, wind, limiter, ratio, growth, whitecap, idxp, spectrum):
    points = spectrum.shape[1]
    runs = points // RUN
    block = RUN
    block_groups = block // SUB
    steps = groups // block_groups
    base = chunk * steps
    whole = lambda i: (0, 0)
    cells = groups * SUB * points

    def body(*refs):
        source_kernel(cap, runs, *refs)

    return pl.pallas_call(
        body,
        grid=(steps,),
        in_specs=[
            pl.BlockSpec(memory_space=pltpu.SMEM),
            pl.BlockSpec((1, points), whole),
            pl.BlockSpec((1, points), whole),
            pl.BlockSpec((SUB, points), whole),
            pl.BlockSpec((1, 1, RUN), lambda i: (base + i, 0, 0)),
            pl.BlockSpec((1, 1, RUN), lambda i: (base + i, 0, 0)),
            pl.BlockSpec((runs, RUN), whole),
            pl.BlockSpec((block, points), lambda i: (base + i, 0)),
        ],
        out_specs=[
            pl.BlockSpec((block, points), lambda i: (i, 0)),
            pl.BlockSpec((block_groups, cap, SUB, RUN), lambda i: (i, 0, 0, 0)),
        ],
        out_shape=[
            jax.ShapeDtypeStruct((groups * SUB, points), jnp.float32),
            jax.ShapeDtypeStruct((groups, cap, SUB, RUN), jnp.float32),
        ],
        cost_estimate=pl.CostEstimate(flops=10 * cells, bytes_accessed=12 * cells, transcendentals=2 * cells),
        compiler_params=pltpu.CompilerParams(vmem_limit_bytes=24 * MIB),
        name="sources",
    )(off, wind, limiter, ratio, growth[:, None, :], whitecap[:, None, :], idxp, spectrum)


def propagate_kernel(
    cap, runs, row_runs, slot, off, info, recv, idxu, idxp, wet, cx, cy, counts, sent, field, other, wide
):
    total = slot.shape[0]
    lane = lanes()
    blank = jnp.zeros((SUB, RUN), jnp.float32)
    for ref in (field, other):
        for q in range(row_runs):
            ref[q] = blank
            ref[row_runs + total + q] = blank

    span = 4 * SUB

    def spread_wet(i, carry):
        t0 = pl.multiple_of(i * span, SUB)
        block = wet[pl.ds(t0, span), :].astype(jnp.float32)
        for j in range(span):
            wide[t0 + j] = rows_of(block, j)
        return carry

    lax.fori_loop(0, total // span, spread_wet, 0)

    def unpack(i, carry):
        t0 = pl.multiple_of(i * runs, SUB)
        base = i * cap
        indices = idxu[pl.ds(t0, runs), :]
        done = []
        for j in range(runs):
            first, start = place(off[t0 + j], cap)
            second = jnp.minimum(first + 1, cap - 1)
            window = jnp.where(lane >= start, recv[base + first], recv[base + second])
            index = rows_of(indices, j)
            cells = lane_gather(window, jnp.bitwise_and(index, RUN - 1))
            done.append(jnp.where(index < RUN, cells, 0.0))
        for j in range(runs):
            field[row_runs + slot[t0 + j]] = done[j]
        return carry

    lax.fori_loop(0, total // runs, unpack, 0)

    up_row = info[0]
    last = info[2]
    block = 32 * row_runs

    def run_steps(eastward):
        edge = lane == (0 if eastward else RUN - 1)
        shift = 1 if eastward else RUN - 1

        def step(n, src, dst):
            on = n < counts[...]
            b = jnp.where(on, cx[...], 0.0)
            c = jnp.where(on, cy[...], 0.0)
            a = 1.0 - b - c

            def rows(i, inner):
                t0 = i * block
                here = src[pl.ds(row_runs + t0, block)]
                up_x = src[pl.ds(row_runs + t0 + up_row, block)]
                sea = wide[pl.ds(t0, block)]
                rolled = [pltpu.roll(here[k], shift, 1) for k in range(block)]
                out = []
                for k in range(block):
                    q = k % row_runs
                    near = rolled[k - q + (q - 1 if eastward else q + 1) % row_runs]
                    up_y = jnp.where(edge, near, rolled[k])
                    out.append(sea[k] * (a * here[k] + b * up_x[k] + c * up_y))
                dst[pl.ds(row_runs + t0, block)] = jnp.stack(out)
                return inner

            lax.fori_loop(0, total // block, rows, 0)

        def pair(m, carry):
            step(2 * m, field, other)
            step(2 * m + 1, other, field)
            return carry

        lax.fori_loop(0, (last + 1) // 2, pair, 0)

    @pl.when(info[1] > 0)
    def _():
        run_steps(True)

    @pl.when(info[1] <= 0)
    def _():
        run_steps(False)

    def pack(i, carry):
        t0 = pl.multiple_of(i * runs, SUB)
        indices = idxp[pl.ds(t0, runs), :]
        picked = [
            lane_gather(field[row_runs + slot[t0 + j]], rows_of(indices, j)) for j in range(runs)
        ]
        spots = [place(off[t0 + j], cap) for j in range(runs)]

        def store(at, value):
            sent[i * cap + at] = value

        write_stream(picked, spots, lane, store, cap)
        return carry

    lax.fori_loop(0, total // runs, pack, 0)


def propagate(cap, runs, row_runs, slot, off, info, recv, idxu, idxp, wet, cx, cy, counts):
    total = slot.shape[0]
    smem = pl.BlockSpec(memory_space=pltpu.SMEM)
    vmem = pl.BlockSpec(memory_space=pltpu.VMEM)
    cells = total * RUN * SUB

    def body(*refs):
        propagate_kernel(cap, runs, row_runs, *refs)

    padded = pltpu.VMEM((total + 2 * row_runs, SUB, RUN), jnp.float32)
    return pl.pallas_call(
        body,
        in_specs=[smem] * 3 + [vmem] * 7,
        out_specs=vmem,
        out_shape=jax.ShapeDtypeStruct(recv.shape, jnp.float32),
        scratch_shapes=[padded, padded, pltpu.VMEM((total, SUB, RUN), jnp.float32)],
        cost_estimate=pl.CostEstimate(flops=100 * cells, bytes_accessed=40 * cells, transcendentals=0),
        compiler_params=pltpu.CompilerParams(vmem_limit_bytes=32 * MIB),
        name="propagate",
    )(slot, off, info, recv, idxu, idxp, wet, cx, cy, counts)


def finish_kernel(cap, runs, comps, steps, begin, end, off, idxu, recv, forced, *rest):
    if begin:
        out, total = rest
    else:
        before, _, out, total = rest
    groups = forced.shape[0] // SUB
    lane = lanes()
    step = pl.program_id(0)

    @pl.when(step == 0)
    def _():
        total[...] = jnp.zeros_like(total) if begin else before[...]

    spots = [place(off[t, 0], cap) for t in range(runs)]
    for g in range(groups):
        rows = slice(g * SUB, (g + 1) * SUB)
        done = []
        for t in range(runs):
            first, start = spots[t]
            index = rows_of(idxu, t)
            window = jnp.where(lane >= start, recv[g, first], recv[g, jnp.minimum(first + 1, cap - 1)])
            cells = lane_gather(window, jnp.bitwise_and(index, RUN - 1))
            done.append(jnp.where(index < RUN, cells, forced[rows, columns(t)]))
        for t in range(runs):
            out[rows, columns(t)] = done[t]
    for t in range(runs):
        cols = columns(t)
        added = [out[g * SUB : (g + 1) * SUB, cols] for g in range(groups)]
        while len(added) > 1:
            added = [sum(added[k : k + 2]) for k in range(0, len(added), 2)]
        total[:, cols] = total[:, cols] + added[0]

    if end:

        @pl.when(step == steps - 1)
        def _():
            mean = jnp.sum(total[...], axis=0, keepdims=True) / comps
            height = 4.0 * jnp.sqrt(mean + 1e-06)
            total[...] = jnp.broadcast_to(height, total.shape)


def finish(cap, comps, chunk, begin, end, off, idxu, recv, forced, before, out):
    points = forced.shape[1]
    runs = points // RUN
    groups = recv.shape[0]
    block_groups = 4
    steps = groups // block_groups
    base = chunk * steps
    whole = lambda i: (0, 0)
    specs = [
        pl.BlockSpec(memory_space=pltpu.SMEM),
        pl.BlockSpec((runs, RUN), whole),
        pl.BlockSpec((block_groups, cap, SUB, RUN), lambda i: (i, 0, 0, 0)),
        pl.BlockSpec((block_groups * SUB, points), lambda i: (i, 0)),
    ]
    args = [off, idxu, recv, forced]
    aliases = {}
    if not begin:
        specs += [pl.BlockSpec((SUB, points), whole), pl.BlockSpec(memory_space=pl.ANY)]
        args += [before, out]
        aliases = {5: 0}
    cells = groups * SUB * points

    def body(*refs):
        finish_kernel(cap, runs, comps, steps, begin, end, *refs)

    return pl.pallas_call(
        body,
        grid=(steps,),
        in_specs=specs,
        out_specs=[
            pl.BlockSpec((block_groups * SUB, points), lambda i: (base + i, 0)),
            pl.BlockSpec((SUB, points), whole),
        ],
        out_shape=[
            jax.ShapeDtypeStruct((comps, points), jnp.float32),
            jax.ShapeDtypeStruct((SUB, points), jnp.float32),
        ],
        input_output_aliases=aliases,
        cost_estimate=pl.CostEstimate(flops=4 * cells, bytes_accessed=12 * cells, transcendentals=0),
        compiler_params=pltpu.CompilerParams(vmem_limit_bytes=16 * MIB),
        name="finish",
    )(*args)


def packed(spectrum, wind, growth, whitecap, courant, substeps, limiter, deck, wet):
    axes = ("pt", "comp")
    comp_count = lax.axis_size("comp")
    devices = lax.axis_size("pt") * comp_count
    rank = lax.axis_index("pt") * comp_count + lax.axis_index("comp")
    comps, points = spectrum.shape
    runs = points // RUN
    total = deck.shape[0] // RUN
    row_runs = wet.shape[1] // RUN
    chunks = comps // (devices * SUB)
    small = (runs * 25 + 31) // 32

    deck = deck.reshape(total, RUN)
    wind = wind[None, :]
    limiter = limiter[None, :]
    growth = growth.reshape(comps // RUN, RUN)
    whitecap = whitecap.reshape(comps // RUN, RUN)
    forced, sent_small, sent_full, idxu, idxp, offs, own_idxu, own_idxp, own_off, ratio, need = begin(
        small, runs, row_runs, devices, rank[None].astype(jnp.int32), deck, wet, wind, limiter,
        growth, whitecap, spectrum,
    )

    def branch(cap, first):
        def run(spectrum):
            kept = [forced]
            received = [
                lax.all_to_all(
                    first.reshape(devices, cap, SUB, RUN), axes, split_axis=0, concat_axis=0, tiled=True
                )
            ]
            for chunk in range(1, chunks):
                held, sent = sources(
                    cap, chunk, devices, own_off, wind, limiter, ratio, growth, whitecap, own_idxp, spectrum
                )
                kept.append(held)
                received.append(lax.all_to_all(sent, axes, split_axis=0, concat_axis=0, tiled=True))
            slot = deck[:, 0] // RUN
            off = offs[:, 0]
            wet_runs = wet.reshape(total, RUN)
            returned = []
            for chunk in range(chunks):
                mine = (chunk * devices + rank) * SUB + jnp.arange(SUB, dtype=jnp.int32)
                cross, along = courants(mine, courant)
                counts = substeps[mine]
                info = jnp.stack(
                    [
                        jnp.where(cross[0] > 0, -row_runs, row_runs),
                        jnp.where(along[0] > 0, 1, -1),
                        jnp.max(counts),
                    ]
                ).astype(jnp.int32)
                wide = lambda v: jnp.broadcast_to(v[:, None], (SUB, RUN))
                sent = propagate(
                    cap, runs, row_runs, slot, off, info, received[chunk].reshape(devices * cap, SUB, RUN),
                    idxu, idxp, wet_runs, wide(jnp.abs(cross)), wide(jnp.abs(along)), wide(counts),
                )
                returned.append(
                    lax.all_to_all(
                        sent.reshape(devices, cap, SUB, RUN), axes, split_axis=0, concat_axis=0, tiled=True
                    )
                )
            out, sums = None, None
            for chunk in range(chunks):
                out, sums = finish(
                    cap, comps, chunk, chunk == 0, chunk == chunks - 1, own_off, own_idxu,
                    returned[chunk], kept[chunk], sums, out,
                )
            return out, sums[0]

        return run

    return lax.cond(need[0] <= small * RUN, branch(small, sent_small), branch(runs, sent_full), spectrum)


def fits(spectrum, deck, wet, devices):
    comps, points = spectrum.shape
    runs = points // RUN
    return (
        comps % (devices * SUB) == 0
        and devices % 16 == 0
        and runs % SUB == 0
        and RUN % runs == 0
        and wet.shape[0] % RUN == 0
        and deck.shape[0] % (RUN * RUN) == 0
    )


def on_device(spectrum, *rest):
    devices = lax.axis_size("pt") * lax.axis_size("comp")
    if fits(spectrum, *rest[-2:], devices):
        return packed(spectrum, *rest)
    return plain(spectrum, *rest)


def solution(mesh):
    in_specs = (
        P(None, ("pt", "comp")),
        P(("pt", "comp")),
        P(),
        P(),
        P(),
        P(),
        P(("pt", "comp")),
        P(),
        P(),
    )
    out_specs = (P(None, ("pt", "comp")), P(("pt", "comp")))
    return jax.shard_map(
        on_device, mesh=mesh, in_specs=in_specs, out_specs=out_specs, check_vma=False
    )
```

time: 801 us -> 356 us (0.44)
  local copies, waits for them, and re-layouts: 260 us -> 31.3 us
  blocking collectives: 186 us -> 0 us
  other arithmetic: 158 us -> 2.89 us
  Pallas kernels: 0 us -> 114 us
  starting transfers between devices: 7.89 us -> 19.3 us
    all_to_all x1 -> x0, blocking collectives: 186 us -> none  [on_device(): lax.all_to_all(slots.reshape(per_device, group_size, point_count), ('pt',...]
    mul x10 -> x0, other arithmetic: 118 us -> none  [the longest x8 112 us: substep(): sea = field_grid * wetness[None, :, :]]
    slice x25 -> x3, local copies, waits for them, and re-layouts: 119 us -> 2.13 us  [the longest x1 0.76 us: run(): off = offs[:, 0]]
    pallas_call x0 -> x6, Pallas kernels: none -> 114 us  [the longest x2 70 us: propagate(): pl.pallas_call(body, in_specs=[smem] * 3 + [vmem] * 7, out_specs=vmem, ou...]
    reshape x6 -> x1, local copies, waits for them, and re-layouts: 59.3 us -> 1.9 us  [run(): wet_runs = wet.reshape(total, RUN)]
    select_n x5 -> x3, other arithmetic: 28.7 us -> 0.04 us  [the longest x2 0.03 us: run(): counts = substeps[mine]]
    gather x5 -> x4, local copies, waits for them, and re-layouts: 27.9 us -> 2.57 us  [the longest x2 1.29 us: run(): counts = substeps[mine]]
    all_to_all x2 -> x0, local copies, waits for them, and re-layouts: 23.3 us -> none  [the longest x1 11.6 us: on_device(): lax.all_to_all(forced.reshape(per_device, group_size, point_count), ('pt'...]
  transfers between devices with their start and end apart: 1 -> 4, of which waited for: 1 -> 4; matrix products, arithmetic and copies ran while one was open for 1% -> 4% of each run, Pallas kernels for 0% -> 24%
where the time goes in v1:
time: 356 us; the launch traced here: 355 us
  waiting for transfers between devices  186 us (52%)
  Pallas kernels  114 us (32%)
  local copies, waits for them, and re-layouts  31.3 us (9%)
  starting transfers between devices  19.3 us (5%)
    all_to_all x2, waiting for transfers between devices, run(): lax.all_to_all(sent.reshape(devices, cap, SUB, RUN), axes, split_axis=0,...  96.9 us
    pallas_call x2, Pallas kernels, propagate(): pl.pallas_call(body, in_specs=[smem] * 3 + [vmem] * 7, out_specs=vmem, ou...  70 us
    all_to_all x1, waiting for transfers between devices, run(): lax.all_to_all(first.reshape(devices, cap, SUB, RUN), axes, split_axis=0,...  65.2 us
    all_to_all x1, waiting for transfers between devices, run(): lax.all_to_all(sent, axes, split_axis=0, concat_axis=0, tiled=True)  23.9 us
    pallas_call x1, Pallas kernels, begin(): pl.pallas_call(body, in_specs=[smem, vmem, vmem, vmem, vmem, vmem, vmem,...  20.9 us
    cond x32, local copies, waits for them, and re-layouts  20.1 us
    pallas_call x2, Pallas kernels, finish(): pl.pallas_call(body, grid=(steps,), in_specs=specs, out_specs=[pl.BlockSp...  17.6 us
    all_to_all x2, starting transfers between devices, run(): lax.all_to_all(sent.reshape(devices, cap, SUB, RUN), axes, split_axis=0,...  7.93 us
  transfers between devices with their start and end apart: 4, of which 4 were waited for; matrix products, arithmetic and copies ran while one was open for 4% of the time, Pallas kernels for 24%

profile of v1, /device:TPU:0, one launch (start us, length us, event | category | flops | bytes accessed | tf_op | source)
XLA Modules:
  0.0 355.1 jit_solution(16747844348524024442)
XLA Ops:
  0.7 20.9 %begin.1 = (f32[256,4096]{1,0:T(8,128)}, f32[800,8,128]{2,1,0:T(8,128)}, f32[1024,8,128]{2,1,0:T(8,128)}, s32[1024,128]{1,0:T(8,128)S(1)}, s32[1024,128]{1,0:T(8...) custom-call(s32[1]{0:T(128)} %bitcast.32.refs_0_, ...), custom_call_target="tpu_custom_call" | custom-call | flops 20971520 | bytes 20971520 | tf_op jit(solution)/shard_map/begin/pallas_call | solution.py:314
  22.3 332.8 %conditional.1 = (f32[512,4096]{1,0:T(8,128)}, f32[4096]{0:T(1024)}) conditional(s32[]{:T(128)} %bitcast.38, (s32[1024,128]{1,0:T(8,128)S(1)}, s32[1024,128]{1,0:T(8,128)S(1)}, s32[]{:T(128)}, f32[16]{0:T(128)S(1)}, s32[512]{0:T(512)S(1)}, /*index=5*/f32[512]{0:T(512)S(1)}, f32[512]{0:T(512)S(1)}, s32[32,128]{1,0:T(8,128)S(1)}, ...), branch_computations={%region_0.3_spmd, %region_3.6_spmd} | conditional | flops 228609696 | bytes 304187456 | solution.py:699
  22.4 0.7 copy-done.18
  23.9 7.3 %all-to-all-start.6 = ((f32[32,25,8,128]{3,2,1,0:T(8,128)}), f32[32,25,8,128]{3,2,1,0:T(8,128)S(1)}, u32[]{:S(2)}, u32[]{:S(2)}) async-start(f32[32,25,8,128]{3,2,1,0:T(8,128)} %bitcast.69), calls=%async_computation.6 | async-start | bytes 6553600 | tf_op jit(solution)/shard_map/cond/branch_1_fun/all_to_all | solution.py:654
  31.2 5.3 %sources.3 = (f32[256,4096]{1,0:T(8,128)S(1)}, f32[32,25,8,128]{3,2,1,0:T(8,128)S(1)}) custom-call(s32[32,128]{1,0:T(8,128)S(1)} %get-tuple-element.101.refs_0_, f32[1,4096]{1,0:T(1,128)S(1)} %get-tuple-element.108.refs_1_, s32[1,4096]{1,0:T(1,128)S(1)} %get-tuple-element.109.refs_2_, f32[8,4096]{1,0:T(8,128)S(1)} %get-tuple-element.110.refs_3_, ...), custom_call_target="tpu_custom_call" | custom-call | flops 10485760 | bytes 12582912 | tf_op jit(solution)/shard_map/cond/branch_1_fun/sources/pallas_call | solution.py:391
  36.5 2.1 copy-done.13
  38.5 1.7 copy-done.15
  40.2 65.2 %all-to-all-done.6 = f32[32,25,8,128]{3,2,1,0:T(8,128)S(1)} async-done(((f32[32,25,8,128]{3,2,1,0:T(8,128)}), f32[32,25,8,128]{3,2,1,0:T(8,128)S(1)}, u32[]{:S(2)}, u32[]{:S(2)}) %all-to-all-start.6) | async-done | bytes 3276832 | tf_op jit(solution)/shard_map/cond/branch_1_fun/all_to_all | solution.py:654
  105.4 1.7 copy-done.5
  107.1 4.1 %all-to-all-start.4 = ((f32[32,25,8,128]{3,2,1,0:T(8,128)}), f32[32,25,8,128]{3,2,1,0:T(8,128)S(1)}, u32[]{:S(2)}, u32[]{:S(2)}) async-start(f32[32,25,8,128]{3,2,1,0:T(8,128)} %copy-done.15), calls=%async_computation.4 | async-start | bytes 6553600 | tf_op jit(solution)/shard_map/cond/branch_1_fun/all_to_all | solution.py:663
  112.1 1.9 reshape.481.refs_6_
  114.0 2.0 copy.18
  116.0 0.8 slice.61
  116.8 2.0 copy.17
  118.8 0.8 slice.60
  121.8 1.9 copy-done.6
  123.8 1.0 copy-done.8
  124.8 35.0 %propagate.7 = f32[800,8,128]{2,1,0:T(8,128)S(1)} custom-call(s32[1024]{0:T(1024)S(1)} %add_select_fusion.1.refs_0_, s32[1024]{0:T(1024)S(1)} %bitcast.63, s32[3]{0:T(128)S(1)} %pad_add_fusion.3.refs_2_, f32[800,8,128]{2,1,0:T(8,128)S(1)} %bitcast.59, s32[1024,128]{1,0:T(8,128)} %copy-done.18, s32[1024,128]{1,0:T(8,128)} %copy-done.19, ...), custom_call_target="tpu_custom_call" | custom-call | flops 104857600 | bytes 41943040 | tf_op jit(solution)/shard_map/cond/branch_1_fun/propagate/pallas_call | solution.py:531
  159.8 1.7 copy-done.4
  161.5 23.9 %all-to-all-done.4 = f32[32,25,8,128]{3,2,1,0:T(8,128)S(1)} async-done(((f32[32,25,8,128]{3,2,1,0:T(8,128)}), f32[32,25,8,128]{3,2,1,0:T(8,128)S(1)}, u32[]{:S(2)}, u32[]{:S(2)}) %all-to-all-start.4) | async-done | bytes 3276832 | tf_op jit(solution)/shard_map/cond/branch_1_fun/all_to_all | solution.py:663
  185.4 1.7 copy-done.2
  187.1 3.9 %all-to-all-start.7 = ((f32[32,25,8,128]{3,2,1,0:T(8,128)}), f32[32,25,8,128]{3,2,1,0:T(8,128)S(1)}, u32[]{:S(2)}, u32[]{:S(2)}) async-start(f32[32,25,8,128]{3,2,1,0:T(8,128)} %bitcast.58), calls=%async_computation.7 | async-start | bytes 6553600 | tf_op jit(solution)/shard_map/cond/branch_1_fun/all_to_all | solution.py:685
  194.1 1.9 copy-done.3
  196.0 1.0 copy-done.9
  197.0 35.0 %propagate.6 = f32[800,8,128]{2,1,0:T(8,128)S(1)} custom-call(s32[1024]{0:T(1024)S(1)} %add_select_fusion.1.refs_0_, s32[1024]{0:T(1024)S(1)} %bitcast.64, s32[3]{0:T(128)S(1)} %pad_add_fusion.2.refs_2_, f32[800,8,128]{2,1,0:T(8,128)S(1)} %bitcast.57, s32[1024,128]{1,0:T(8,128)} %copy-done.18, s32[1024,128]{1,0:T(8,128)} %copy-done.19, ...), custom_call_target="tpu_custom_call" | custom-call | flops 104857600 | bytes 41943040 | tf_op jit(solution)/shard_map/cond/branch_1_fun/propagate/pallas_call | solution.py:531
  232.1 1.7 copy-done.7
  233.7 31.5 %all-to-all-done.7.refs_2_ = f32[32,25,8,128]{3,2,1,0:T(8,128)S(1)} async-done(((f32[32,25,8,128]{3,2,1,0:T(8,128)}), f32[32,25,8,128]{3,2,1,0:T(8,128)S(1)}, u32[]{:S(2)}, u32[]{:S(2)}) %all-to-all-start.7) | async-done | bytes 3276832 | tf_op jit(solution)/shard_map/cond/branch_1_fun/all_to_all | solution.py:685
  265.3 4.1 %all-to-all-start.5 = ((f32[32,25,8,128]{3,2,1,0:T(8,128)}), f32[32,25,8,128]{3,2,1,0:T(8,128)}, u32[]{:S(2)}, u32[]{:S(2)}) async-start(f32[32,25,8,128]{3,2,1,0:T(8,128)} %bitcast.60), calls=%async_computation.5 | async-start | bytes 6553600 | tf_op jit(solution)/shard_map/cond/branch_1_fun/all_to_all | solution.py:685
  269.3 8.8 %finish.6 = (f32[512,4096]{1,0:T(8,128)}, f32[8,4096]{1,0:T(8,128)S(1)}) custom-call(s32[32,128]{1,0:T(8,128)S(1)} %get-tuple-element.101.refs_0_, s32[32,128]{1,0:T(8,128)S(1)} %get-tuple-element.102.refs_1_, f32[32,25,8,128]{3,2,1,0:T(8,128)S(1)} %all-to-all-done.7.refs_2_, f32[256,4096]{1,0:T(8,128)} %get-tuple-element.121.refs_3_), custom_call_target="tpu_custom_call" | custom-call | flops 4194304 | bytes 12582912 | tf_op jit(solution)/shard_map/cond/branch_1_fun/finish/pallas_call | solution.py:609
  278.2 65.4 %all-to-all-done.5.refs_2_ = f32[32,25,8,128]{3,2,1,0:T(8,128)} async-done(((f32[32,25,8,128]{3,2,1,0:T(8,128)}), f32[32,25,8,128]{3,2,1,0:T(8,128)}, u32[]{:S(2)}, u32[]{:S(2)}) %all-to-all-start.5) | async-done | bytes 3276832 | tf_op jit(solution)/shard_map/cond/branch_1_fun/all_to_all | solution.py:685
  343.6 2.2 copy-done.14
  345.8 8.7 %finish.7 = (f32[512,4096]{1,0:T(8,128)}, f32[8,4096]{1,0:T(8,128)S(1)}) custom-call(s32[32,128]{1,0:T(8,128)S(1)} %get-tuple-element.101.refs_0_, s32[32,128]{1,0:T(8,128)S(1)} %get-tuple-element.102.refs_1_, f32[32,25,8,128]{3,2,1,0:T(8,128)} %all-to-all-done.5.refs_2_, f32[256,4096]{1,0:T(8,128)S(1)} %copy-done.14, ...), custom_call_target="tpu_custom_call", output_to_operand_aliasing={{0}: (5, {})} | custom-call | flops 4194304 | bytes 12582912 | tf_op jit(solution)/shard_map/cond/branch_1_fun/finish/pallas_call | solution.py:609
  (60 shorter events, 7.3 us)
Async XLA Ops:
  0.6 21.6 %copy-start.16 = (f32[16]{0:T(128)S(1)}, f32[16]{0:T(128)}, u32[]{:S(2)}) copy-start(f32[16]{0:T(128)} %param.15) | copy-start | bytes 196
  0.6 21.6 %copy-start.17 = (s32[512]{0:T(512)S(1)}, s32[512]{0:T(512)}, u32[]{:S(2)}) copy-start(s32[512]{0:T(512)} %param.16) | copy-start | bytes 6148
  0.7 21.6 %copy-start.20 = (s32[131072]{0:T(1024)S(1)}, s32[131072]{0:T(1024)}, u32[]{:S(2)}) copy-start(s32[131072]{0:T(1024)} %param.18) | copy-start | bytes 1572868
  0.7 21.6 %copy-start.22 = (s32[256,512]{1,0:T(8,128)S(1)}, s32[256,512]{1,0:T(8,128)}, u32[]{:S(2)}) copy-start(s32[256,512]{1,0:T(8,128)} %refs_2_.1) | copy-start | bytes 1572868
  0.7 21.6 %copy-start.25 = (f32[4096]{0:T(1024)S(1)}, f32[4096]{0:T(1024)}, u32[]{:S(2)}) copy-start(f32[4096]{0:T(1024)} %param.12) | copy-start | bytes 49156
  0.7 21.6 %copy-start.26 = (s32[4096]{0:T(1024)S(1)}, s32[4096]{0:T(1024)}, u32[]{:S(2)}) copy-start(s32[4096]{0:T(1024)} %param.17) | copy-start | bytes 49156
  0.7 21.6 %copy-start.27 = (f32[512]{0:T(512)S(1)}, f32[512]{0:T(512)}, u32[]{:S(2)}) copy-start(f32[512]{0:T(512)} %param.13) | copy-start | bytes 6148
  0.7 21.6 %copy-start.28 = (f32[512]{0:T(512)S(1)}, f32[512]{0:T(512)}, u32[]{:S(2)}) copy-start(f32[512]{0:T(512)} %param.14) | copy-start | bytes 6148
  22.4 0.8 copy-start.18
  22.4 1.0 copy-start.19
  22.4 1.2 copy-start.21
  22.4 1.3 copy-start.23
  22.4 1.5 copy-start.24
  23.9 81.6 %all-to-all-start.6 = ((f32[32,25,8,128]{3,2,1,0:T(8,128)}), f32[32,25,8,128]{3,2,1,0:T(8,128)S(1)}, u32[]{:S(2)}, u32[]{:S(2)}) async-start(f32[32,25,8,128]{3,2,1,0:T(8,128)} %bitcast.69), calls=%async_computation.6 | async-start | bytes 6553600 | tf_op jit(solution)/shard_map/cond/branch_1_fun/all_to_all | solution.py:654
  36.4 2.1 copy-start.13
  38.5 1.7 copy-start.15
  105.4 1.7 copy-start.5
  107.1 78.3 %all-to-all-start.4 = ((f32[32,25,8,128]{3,2,1,0:T(8,128)}), f32[32,25,8,128]{3,2,1,0:T(8,128)S(1)}, u32[]{:S(2)}, u32[]{:S(2)}) async-start(f32[32,25,8,128]{3,2,1,0:T(8,128)} %copy-done.15), calls=%async_computation.4 | async-start | bytes 6553600 | tf_op jit(solution)/shard_map/cond/branch_1_fun/all_to_all | solution.py:663
  121.8 1.9 copy-start.6
  123.8 1.0 copy-start.8
  159.8 1.7 copy-start.4
  185.4 1.7 copy-start.2
  187.1 78.1 %all-to-all-start.7 = ((f32[32,25,8,128]{3,2,1,0:T(8,128)}), f32[32,25,8,128]{3,2,1,0:T(8,128)S(1)}, u32[]{:S(2)}, u32[]{:S(2)}) async-start(f32[32,25,8,128]{3,2,1,0:T(8,128)} %bitcast.58), calls=%async_computation.7 | async-start | bytes 6553600 | tf_op jit(solution)/shard_map/cond/branch_1_fun/all_to_all | solution.py:685
  194.1 1.9 copy-start.3
  196.0 1.0 copy-start.9
  232.1 1.7 copy-start.7
  265.3 78.3 %all-to-all-start.5 = ((f32[32,25,8,128]{3,2,1,0:T(8,128)}), f32[32,25,8,128]{3,2,1,0:T(8,128)}, u32[]{:S(2)}, u32[]{:S(2)}) async-start(f32[32,25,8,128]{3,2,1,0:T(8,128)} %bitcast.60), calls=%async_computation.5 | async-start | bytes 6553600 | tf_op jit(solution)/shard_map/cond/branch_1_fun/all_to_all | solution.py:685
  343.6 2.2 copy-start.14

commit v2 on v1

--- a/solution.py
+++ b/solution.py
@@ -15,7 +15,8 @@
 rate_limit = 0.5
 time_step = 0.5
 
-MIB = 1024 * 1024
+FINISH_PARTS = 8
+VMEM_GRANT = 60 * 1024 * 1024
 
 
 def plain_sources(spectrum, wind, growth, whitecap, limiter):
@@ -148,24 +149,15 @@
     return jnp.transpose(jnp.broadcast_to(row, (RUN, RUN)))
 
 
-def begin_kernel(
-    small, runs, row_runs, rank, deck, wet, wind, limiter, growth, whitecap, spectrum,
-    held, sent_small, sent_full, idxu, idxp, offs, own_idxu, own_idxp, own_off, ratio, need,
-    values, packed, sea, total, grown, capped, off, in_sems, held_sems, sent_sems, off_sem,
-):
-    comps = values.shape[0]
-    slots = deck.shape[0]
-    groups = packed.shape[0] // runs
-    parts = in_sems.shape[0]
-    part = comps // parts
-
-    def fetch(p):
-        rows = pl.ds(p * part, part)
-        return pltpu.make_async_copy(spectrum.at[rows], values.at[rows], in_sems.at[p])
-
-    for p in range(parts):
-        fetch(p).start()
-
+def dot(a, b):
+    return jnp.dot(a, b, preferred_element_type=jnp.float32)
+
+
+def one(mask):
+    return jnp.where(mask, 1.0, 0.0).astype(jnp.bfloat16)
+
+
+def lay_out(wet, sea, row_runs):
     halves = wet.shape[0] // RUN
     for q in range(row_runs):
         for h in range(halves):
@@ -174,50 +166,78 @@
                 jnp.float32
             ).astype(jnp.bfloat16)
 
-    lane = lanes(RUN)
-    row = lax.broadcasted_iota(jnp.int32, (RUN, RUN), 0)
-    one = lambda mask: jnp.where(mask, 1.0, 0.0).astype(jnp.bfloat16)
-    earlier = one(row < lane)
-    ones = jnp.ones((RUN, RUN), jnp.bfloat16)
-    runs_before = one((lane < row) & (lane // runs == row // runs))
-    dot = lambda a, b: jnp.dot(a, b, preferred_element_type=jnp.float32)
-
-    def tables(b, most):
-        here = pl.ds(pl.multiple_of(b * RUN, RUN), RUN)
-        slot = deck[here, :] // RUN
-        picks = [
+
+def picks(slot, row_runs, halves):
+    lane = lanes(slot.shape[0])
+    return jnp.concatenate(
+        [
             one(slot == lane * row_runs + (h * RUN * row_runs + q))
             for q in range(row_runs)
             for h in range(halves)
-        ]
-        wet_here = dot(jnp.concatenate(picks, axis=1), sea[...])
-        wet_low = wet_here.astype(jnp.bfloat16)
-        prefix = dot(wet_low, earlier)
-        count = dot(wet_low, ones)
-        off_f = dot(runs_before, count.astype(jnp.bfloat16))
-        off_i = off_f.astype(jnp.int32)
-        through = (prefix + wet_here).astype(jnp.int32)
-        spot = jnp.bitwise_and(off_i + prefix.astype(jnp.int32), RUN - 1)
-        idxu[here, :] = jnp.where(wet_here > 0.5, spot, spot + RUN)
-        offs[here, :] = off_i
-        nth = jnp.bitwise_and(lane - off_i, RUN - 1)
-        at = jnp.zeros((RUN, RUN), jnp.int32)
-        bit = RUN // 2
-        while bit:
-            probe = lane_gather(through, at + (bit - 1))
-            at = jnp.where(probe <= nth, at + bit, at)
-            bit //= 2
-        idxp[here, :] = at
-        return jnp.maximum(most, jnp.max(off_f + count))
-
-    most = lax.fori_loop(0, slots // RUN, tables, jnp.float32(0)).astype(jnp.int32)
-    need[0] = most
+        ],
+        axis=1,
+    )
+
+
+def stream_tables(wet_here, before):
+    lane = lanes(wet_here.shape[0])
+    wet_low = wet_here.astype(jnp.bfloat16)
+    square = lambda: (lax.broadcasted_iota(jnp.int32, (RUN, RUN), 0), lanes(RUN))
+    row, column = square()
+    prefix = dot(wet_low, one(row < column))
+    count = dot(wet_low, jnp.ones((RUN, RUN), jnp.bfloat16))
+    off = dot(before, count.astype(jnp.bfloat16)).astype(jnp.int32)
+    through = (prefix + wet_here).astype(jnp.int32)
+    spot = jnp.bitwise_and(off + prefix.astype(jnp.int32), RUN - 1)
+    idxu = jnp.where(wet_here > 0.5, spot, spot + RUN)
+    nth = jnp.bitwise_and(lane - off, RUN - 1)
+    at = jnp.zeros(nth.shape, jnp.int32)
+    bit = RUN // 2
+    while bit:
+        probe = lane_gather(through, at + (bit - 1))
+        at = jnp.where(probe <= nth, at + bit, at)
+        bit //= 2
+    return off, idxu, at
+
+
+def begin_kernel(
+    small, runs, row_runs, rank, deck, wet, wind, limiter, growth, whitecap, spectrum,
+    sent_small, sent_full, own_idxu, own_idxp, own_off, ratio, need,
+    values, packed, sea, total, grown, capped, off, in_sems, sent_sems, off_sem,
+):
+    comps = values.shape[0]
+    slots = deck.shape[0]
+    groups = packed.shape[0]
+    parts = in_sems.shape[0]
+    part = comps // parts
+
+    def fetch(p):
+        rows = pl.ds(p * part, part)
+        return pltpu.make_async_copy(spectrum.at[rows], values.at[rows], in_sems.at[p])
+
+    for p in range(parts):
+        fetch(p).start()
+
+    halves = wet.shape[0] // RUN
+    lay_out(wet, sea, row_runs)
+    ones = jnp.ones((RUN, RUN), jnp.bfloat16)
+
     mine = pl.ds(pl.multiple_of(rank[0] * runs, SUB), runs)
-    own_idxu[...] = idxu[mine, :]
-    own_idxp[...] = idxp[mine, :]
-    own_off[...] = offs[mine, :]
+    wet_mine = dot(picks(deck[mine, :] // RUN, row_runs, halves), sea[...])
+    below = lax.broadcasted_iota(jnp.int32, (runs, runs), 1) < lax.broadcasted_iota(jnp.int32, (runs, runs), 0)
+    own_off[...], own_idxu[...], own_idxp[...] = stream_tables(wet_mine, one(below))
     off_copy = pltpu.make_async_copy(own_off, off, off_sem)
     off_copy.start()
+
+    same = one(lanes(RUN) // runs == lax.broadcasted_iota(jnp.int32, (RUN, RUN), 0) // runs)
+    counts = dot(sea[...], ones).astype(jnp.bfloat16)
+    most = None
+    for b in range(slots // RUN):
+        here = dot(picks(deck[b * RUN : (b + 1) * RUN, :] // RUN, row_runs, halves), counts)
+        sums = dot(same, here.astype(jnp.bfloat16))
+        most = sums if most is None else jnp.maximum(most, sums)
+    most = jnp.max(most).astype(jnp.int32)
+    need[0] = most
 
     for r in range(grown.shape[0] // RUN):
         rows = slice(r * RUN, (r + 1) * RUN)
@@ -236,64 +256,60 @@
     ratio[...] = jnp.broadcast_to(mean / (1.0 + mean), ratio.shape)
 
     off_copy.wait()
-    cap = jnp.where(most <= small * RUN, small, runs)
+    fits_small = most <= small * RUN
+    cap = jnp.where(fits_small, small, runs)
     reg_lane = lanes()
-
-    def keep(g):
-        rows = pl.ds(pl.multiple_of(g * SUB, SUB), SUB)
-        return pltpu.make_async_copy(values.at[rows], held.at[rows], held_sems.at[g])
-
-    def pass_on(g, size, target):
-        regs = pl.ds(g * size, size)
-        return pltpu.make_async_copy(packed.at[regs], target.at[regs], sent_sems.at[g])
-
-    def group(g, carry):
-        rows = pl.ds(pl.multiple_of(g * SUB, SUB), SUB)
-        growth_g = grown[rows, :]
-        whitecap_g = capped[rows, :]
-        forced = []
-        for t in range(runs):
-            cols = columns(t)
-            wind_t = jnp.broadcast_to(wind[:, cols], (SUB, RUN))
-            limited = jnp.broadcast_to(limiter[:, cols], (SUB, RUN)) == 1
-            forced.append(force(values[rows, cols], wind_t, ratio[:, cols], limited, growth_g, whitecap_g))
-        for t in range(runs):
-            values[rows, columns(t)] = forced[t]
-        keep(g).start()
-        sent = [lane_gather(forced[t], rows_of(own_idxp, t)) for t in range(runs)]
+    several = 8
+    tall = several * SUB
+
+    def pass_on(i, size, target):
+        these = pl.ds(i * several, several)
+        return pltpu.make_async_copy(packed.at[these, pl.ds(0, size)], target.at[these], sent_sems.at[i])
+
+    def some(i, carry):
         spots = [place(off[t, 0], cap) for t in range(runs)]
-
-        def store(at, value):
-            packed[g * cap + at] = value
-
-        write_stream(sent, spots, reg_lane, store, cap)
-
-        @pl.when(most <= small * RUN)
+        here = packed.at[pl.ds(i * several, several)]
+        for g in range(several):
+            rows = pl.ds(pl.multiple_of(i * tall + g * SUB, SUB), SUB)
+            forced = []
+            for t in range(runs):
+                cols = columns(t)
+                wind_t = jnp.broadcast_to(wind[:, cols], (SUB, RUN))
+                limited = jnp.broadcast_to(limiter[:, cols], (SUB, RUN)) == 1
+                forced.append(
+                    force(values[rows, cols], wind_t, ratio[:, cols], limited, grown[rows, :], capped[rows, :])
+                )
+            sent = [lane_gather(forced[t], rows_of(own_idxp, t)) for t in range(runs)]
+
+            def store(at, value, g=g):
+                here[g, at] = value
+
+            write_stream(sent, spots, reg_lane, store, cap)
+
+        @pl.when(fits_small)
         def _():
-            pass_on(g, small, sent_small).start()
-
-        @pl.when(most > small * RUN)
+            pass_on(i, small, sent_small).start()
+
+        @pl.when(jnp.logical_not(fits_small))
         def _():
-            pass_on(g, runs, sent_full).start()
+            pass_on(i, runs, sent_full).start()
 
         return carry
 
-    lax.fori_loop(0, groups, group, 0)
-
-    def drain(g, carry):
-        keep(g).wait()
-
-        @pl.when(most <= small * RUN)
+    lax.fori_loop(0, groups // several, some, 0)
+
+    def drain(i, carry):
+        @pl.when(fits_small)
         def _():
-            pass_on(g, small, sent_small).wait()
-
-        @pl.when(most > small * RUN)
+            pass_on(i, small, sent_small).wait()
+
+        @pl.when(jnp.logical_not(fits_small))
         def _():
-            pass_on(g, runs, sent_full).wait()
+            pass_on(i, runs, sent_full).wait()
 
         return carry
 
-    lax.fori_loop(0, groups, drain, 0)
+    lax.fori_loop(0, groups // several, drain, 0)
 
 
 def begin(small, runs, row_runs, groups, rank, deck, wet, wind, limiter, growth, whitecap, spectrum):
@@ -303,7 +319,7 @@
     parts = 8
     smem = pl.BlockSpec(memory_space=pltpu.SMEM)
     vmem = pl.BlockSpec(memory_space=pltpu.VMEM)
-    far = pl.BlockSpec(memory_space=pl.ANY)
+    far = pl.BlockSpec(memory_space=pltpu.HBM)
     cells = comps * points
     f32 = lambda *shape: jax.ShapeDtypeStruct(shape, jnp.float32)
     i32 = lambda *shape: jax.ShapeDtypeStruct(shape, jnp.int32)
@@ -314,14 +330,10 @@
     return pl.pallas_call(
         body,
         in_specs=[smem, vmem, vmem, vmem, vmem, vmem, vmem, far],
-        out_specs=[far] * 3 + [vmem] * 7 + [smem],
+        out_specs=[far] * 2 + [vmem] * 4 + [smem],
         out_shape=[
-            f32(block, points),
-            f32(groups * small, SUB, RUN),
-            f32(groups * runs, SUB, RUN),
-            i32(slots, RUN),
-            i32(slots, RUN),
-            i32(slots, RUN),
+            f32(groups, small, SUB, RUN),
+            f32(groups, runs, SUB, RUN),
             i32(runs, RUN),
             i32(runs, RUN),
             i32(runs, RUN),
@@ -330,7 +342,7 @@
         ],
         scratch_shapes=[
             pltpu.VMEM((comps, points), jnp.float32),
-            pltpu.VMEM((groups * runs, SUB, RUN), jnp.float32),
+            pltpu.VMEM((groups, runs, SUB, RUN), jnp.float32),
             pltpu.VMEM((slots, RUN), jnp.bfloat16),
             pltpu.VMEM((SUB, points), jnp.float32),
             pltpu.VMEM((block, RUN), jnp.float32),
@@ -338,20 +350,58 @@
             pltpu.SMEM((runs, RUN), jnp.int32),
             pltpu.SemaphoreType.DMA((parts,)),
             pltpu.SemaphoreType.DMA((groups,)),
-            pltpu.SemaphoreType.DMA((groups,)),
             pltpu.SemaphoreType.DMA,
         ],
         cost_estimate=pl.CostEstimate(flops=10 * cells, bytes_accessed=10 * cells, transcendentals=cells),
-        compiler_params=pltpu.CompilerParams(vmem_limit_bytes=32 * MIB),
+        compiler_params=pltpu.CompilerParams(vmem_limit_bytes=VMEM_GRANT),
         name="begin",
     )(rank, deck, wet, wind, limiter, growth, whitecap, spectrum)
 
 
-def source_kernel(cap, runs, off, wind, limiter, ratio, growth, whitecap, idxp, spectrum, forced, packed):
+def tables_kernel(runs, row_runs, deck, wet, idxu, idxp, off, slot, sea):
+    lay_out(wet, sea, row_runs)
+    row = lax.broadcasted_iota(jnp.int32, (RUN, RUN), 0)
+    lane = lanes(RUN)
+    before = one((lane < row) & (lane // runs == row // runs))
+    halves = wet.shape[0] // RUN
+
+    def block(b, carry):
+        here = pl.ds(pl.multiple_of(b * RUN, RUN), RUN)
+        slot_b = deck[here, :] // RUN
+        off_b, idxu[here, :], idxp[here, :] = stream_tables(
+            dot(picks(slot_b, row_runs, halves), sea[...]), before
+        )
+        off[pl.ds(b, 1), :] = jnp.transpose(off_b)[:1, :]
+        slot[pl.ds(b, 1), :] = jnp.transpose(slot_b)[:1, :]
+        return carry
+
+    lax.fori_loop(0, deck.shape[0] // RUN, block, 0)
+
+
+def tables(runs, row_runs, deck, wet):
+    slots = deck.shape[0]
+    vmem = pl.BlockSpec(memory_space=pltpu.VMEM)
+    i32 = lambda *shape: jax.ShapeDtypeStruct(shape, jnp.int32)
+
+    def body(*refs):
+        tables_kernel(runs, row_runs, *refs)
+
+    return pl.pallas_call(
+        body,
+        in_specs=[vmem, vmem],
+        out_specs=[vmem] * 4,
+        out_shape=[i32(slots, RUN), i32(slots, RUN), i32(slots // RUN, RUN), i32(slots // RUN, RUN)],
+        scratch_shapes=[pltpu.VMEM((slots, RUN), jnp.bfloat16)],
+        cost_estimate=pl.CostEstimate(flops=2 * slots * slots * RUN, bytes_accessed=16 * slots * RUN, transcendentals=0),
+        compiler_params=pltpu.CompilerParams(vmem_limit_bytes=VMEM_GRANT),
+        name="tables",
+    )(deck, wet)
+
+
+def source_kernel(cap, runs, off, wind, limiter, ratio, growth, whitecap, idxp, spectrum, forced, *packed):
     groups = spectrum.shape[0] // SUB
     lane = lanes()
     block = groups * SUB
-    step = pl.program_id(0)
     grown = spread(growth[...].reshape(1, RUN))
     capped = spread(whitecap[...].reshape(1, RUN))
     spots = [place(off[t, 0], cap) for t in range(runs)]
@@ -367,15 +417,16 @@
             )
         for t in range(runs):
             forced[rows, columns(t)] = values[t]
-        sent = [lane_gather(values[t], rows_of(idxp, t)) for t in range(runs)]
-
-        def store(at, value, g=g):
-            packed[g, at] = value
-
-        write_stream(sent, spots, lane, store, cap)
-
-
-def sources(cap, chunk, groups, off, wind, limiter, ratio, growth, whitecap, idxp, spectrum):
+        if packed:
+            sent = [lane_gather(values[t], rows_of(idxp, t)) for t in range(runs)]
+
+            def store(at, value, g=g):
+                packed[0][g, at] = value
+
+            write_stream(sent, spots, lane, store, cap)
+
+
+def sources(cap, chunk, groups, pack, off, wind, limiter, ratio, growth, whitecap, idxp, spectrum):
     points = spectrum.shape[1]
     runs = points // RUN
     block = RUN
@@ -404,13 +455,13 @@
         out_specs=[
             pl.BlockSpec((block, points), lambda i: (i, 0)),
             pl.BlockSpec((block_groups, cap, SUB, RUN), lambda i: (i, 0, 0, 0)),
-        ],
+        ][: 1 + pack],
         out_shape=[
-            jax.ShapeDtypeStruct((groups * SUB, points), jnp.float32),
-            jax.ShapeDtypeStruct((groups, cap, SUB, RUN), jnp.float32),
-        ],
+            pltpu.HBM((groups * SUB, points), jnp.float32),
+            pltpu.HBM((groups, cap, SUB, RUN), jnp.float32),
+        ][: 1 + pack],
         cost_estimate=pl.CostEstimate(flops=10 * cells, bytes_accessed=12 * cells, transcendentals=2 * cells),
-        compiler_params=pltpu.CompilerParams(vmem_limit_bytes=24 * MIB),
+        compiler_params=pltpu.CompilerParams(vmem_limit_bytes=VMEM_GRANT),
         name="sources",
     )(off, wind, limiter, ratio, growth[:, None, :], whitecap[:, None, :], idxp, spectrum)
 
@@ -535,92 +586,119 @@
         out_shape=jax.ShapeDtypeStruct(recv.shape, jnp.float32),
         scratch_shapes=[padded, padded, pltpu.VMEM((total, SUB, RUN), jnp.float32)],
         cost_estimate=pl.CostEstimate(flops=100 * cells, bytes_accessed=40 * cells, transcendentals=0),
-        compiler_params=pltpu.CompilerParams(vmem_limit_bytes=32 * MIB),
+        compiler_params=pltpu.CompilerParams(vmem_limit_bytes=VMEM_GRANT),
         name="propagate",
     )(slot, off, info, recv, idxu, idxp, wet, cx, cy, counts)
 
 
-def finish_kernel(cap, runs, comps, steps, begin, end, off, idxu, recv, forced, *rest):
+def finish_kernel(cap, runs, comps, base, begin, end, off, idxu, recv, forced, *rest):
     if begin:
-        out, total = rest
+        out, total, streams, values, stream_sems, value_sems, out_sems = rest
     else:
-        before, _, out, total = rest
-    groups = forced.shape[0] // SUB
+        before, _, out, total, streams, values, stream_sems, value_sems, out_sems = rest
     lane = lanes()
-    step = pl.program_id(0)
-
-    @pl.when(step == 0)
-    def _():
-        total[...] = jnp.zeros_like(total) if begin else before[...]
-
-    spots = [place(off[t, 0], cap) for t in range(runs)]
-    for g in range(groups):
-        rows = slice(g * SUB, (g + 1) * SUB)
-        done = []
-        for t in range(runs):
-            first, start = spots[t]
-            index = rows_of(idxu, t)
-            window = jnp.where(lane >= start, recv[g, first], recv[g, jnp.minimum(first + 1, cap - 1)])
-            cells = lane_gather(window, jnp.bitwise_and(index, RUN - 1))
-            done.append(jnp.where(index < RUN, cells, forced[rows, columns(t)]))
-        for t in range(runs):
-            out[rows, columns(t)] = done[t]
-    for t in range(runs):
-        cols = columns(t)
-        added = [out[g * SUB : (g + 1) * SUB, cols] for g in range(groups)]
-        while len(added) > 1:
-            added = [sum(added[k : k + 2]) for k in range(0, len(added), 2)]
-        total[:, cols] = total[:, cols] + added[0]
-
+    parts = stream_sems.shape[0]
+    groups = recv.shape[0] // parts
+    tall = groups * SUB
+
+    def arrive(p):
+        some = pl.ds(p * groups, groups)
+        return pltpu.make_async_copy(recv.at[some], streams.at[some], stream_sems.at[p])
+
+    def bring(p):
+        rows = pl.ds(pl.multiple_of(p * tall, SUB), tall)
+        return pltpu.make_async_copy(forced.at[rows], values.at[rows], value_sems.at[p])
+
+    def leave(p):
+        rows = pl.ds(pl.multiple_of(p * tall, SUB), tall)
+        there = pl.ds(pl.multiple_of(base + p * tall, SUB), tall)
+        return pltpu.make_async_copy(values.at[rows], out.at[there], out_sems.at[p])
+
+    for p in range(parts):
+        arrive(p).start()
+        bring(p).start()
+    total[...] = jnp.zeros_like(total) if begin else before[...]
+
+    def some(p, carry):
+        arrive(p).wait()
+        bring(p).wait()
+        here = streams.at[pl.ds(p * groups, groups)]
+        block = values.at[pl.ds(pl.multiple_of(p * tall, SUB), tall)]
+        rows = [slice(g * SUB, (g + 1) * SUB) for g in range(groups)]
+        for t0 in range(0, runs, SUB):
+            done = []
+            for t in range(t0, t0 + SUB):
+                first, start = place(off[t, 0], cap)
+                second = jnp.minimum(first + 1, cap - 1)
+                index = rows_of(idxu, t)
+                sea = index < RUN
+                index = jnp.bitwise_and(index, RUN - 1)
+                lower = lane >= start
+                cells = [
+                    lane_gather(jnp.where(lower, here[g, first], here[g, second]), index) for g in range(groups)
+                ]
+                done.append([jnp.where(sea, cells[g], block[rows[g], columns(t)]) for g in range(groups)])
+            for k, settled in enumerate(done):
+                cols = columns(t0 + k)
+                added = total[:, cols]
+                for g in range(groups):
+                    block[rows[g], cols] = settled[g]
+                    added = added + settled[g]
+                total[:, cols] = added
+        leave(p).start()
+        return carry
+
+    lax.fori_loop(0, parts, some, 0)
     if end:
-
-        @pl.when(step == steps - 1)
-        def _():
-            mean = jnp.sum(total[...], axis=0, keepdims=True) / comps
-            height = 4.0 * jnp.sqrt(mean + 1e-06)
-            total[...] = jnp.broadcast_to(height, total.shape)
+        mean = jnp.sum(total[...], axis=0, keepdims=True) / comps
+        height = 4.0 * jnp.sqrt(mean + 1e-06)
+        total[...] = jnp.broadcast_to(height, total.shape)
+
+    def drain(p, carry):
+        leave(p).wait()
+        return carry
+
+    lax.fori_loop(0, parts, drain, 0)
 
 
 def finish(cap, comps, chunk, begin, end, off, idxu, recv, forced, before, out):
-    points = forced.shape[1]
+    block, points = forced.shape
     runs = points // RUN
-    groups = recv.shape[0]
-    block_groups = 4
-    steps = groups // block_groups
-    base = chunk * steps
-    whole = lambda i: (0, 0)
-    specs = [
-        pl.BlockSpec(memory_space=pltpu.SMEM),
-        pl.BlockSpec((runs, RUN), whole),
-        pl.BlockSpec((block_groups, cap, SUB, RUN), lambda i: (i, 0, 0, 0)),
-        pl.BlockSpec((block_groups * SUB, points), lambda i: (i, 0)),
-    ]
+    parts = FINISH_PARTS
+    smem = pl.BlockSpec(memory_space=pltpu.SMEM)
+    whole = lambda *shape: pl.BlockSpec(shape, lambda i: (0, 0))
+    far = pl.BlockSpec(memory_space=pltpu.HBM)
+    specs = [smem, whole(runs, RUN), far, far]
     args = [off, idxu, recv, forced]
     aliases = {}
     if not begin:
-        specs += [pl.BlockSpec((SUB, points), whole), pl.BlockSpec(memory_space=pl.ANY)]
+        specs += [whole(SUB, points), far]
         args += [before, out]
         aliases = {5: 0}
-    cells = groups * SUB * points
+    cells = block * points
 
     def body(*refs):
-        finish_kernel(cap, runs, comps, steps, begin, end, *refs)
+        finish_kernel(cap, runs, comps, chunk * block, begin, end, *refs)
 
     return pl.pallas_call(
         body,
-        grid=(steps,),
+        grid=(1,),
         in_specs=specs,
-        out_specs=[
-            pl.BlockSpec((block_groups * SUB, points), lambda i: (base + i, 0)),
-            pl.BlockSpec((SUB, points), whole),
-        ],
+        out_specs=[far, whole(SUB, points)],
         out_shape=[
             jax.ShapeDtypeStruct((comps, points), jnp.float32),
             jax.ShapeDtypeStruct((SUB, points), jnp.float32),
         ],
+        scratch_shapes=[
+            pltpu.VMEM(recv.shape, jnp.float32),
+            pltpu.VMEM((block, points), jnp.float32),
+            pltpu.SemaphoreType.DMA((parts,)),
+            pltpu.SemaphoreType.DMA((parts,)),
+            pltpu.SemaphoreType.DMA((parts,)),
+        ],
         input_output_aliases=aliases,
         cost_estimate=pl.CostEstimate(flops=4 * cells, bytes_accessed=12 * cells, transcendentals=0),
-        compiler_params=pltpu.CompilerParams(vmem_limit_bytes=16 * MIB),
+        compiler_params=pltpu.CompilerParams(vmem_limit_bytes=VMEM_GRANT),
         name="finish",
     )(*args)
 
@@ -642,27 +720,25 @@
     limiter = limiter[None, :]
     growth = growth.reshape(comps // RUN, RUN)
     whitecap = whitecap.reshape(comps // RUN, RUN)
-    forced, sent_small, sent_full, idxu, idxp, offs, own_idxu, own_idxp, own_off, ratio, need = begin(
+    sent_small, sent_full, own_idxu, own_idxp, own_off, ratio, need = begin(
         small, runs, row_runs, devices, rank[None].astype(jnp.int32), deck, wet, wind, limiter,
         growth, whitecap, spectrum,
     )
 
     def branch(cap, first):
         def run(spectrum):
-            kept = [forced]
-            received = [
-                lax.all_to_all(
-                    first.reshape(devices, cap, SUB, RUN), axes, split_axis=0, concat_axis=0, tiled=True
-                )
-            ]
-            for chunk in range(1, chunks):
-                held, sent = sources(
-                    cap, chunk, devices, own_off, wind, limiter, ratio, growth, whitecap, own_idxp, spectrum
+            kept = []
+            received = []
+            for chunk in range(chunks):
+                held, *sent = sources(
+                    cap, chunk, devices, chunk > 0, own_off, wind, limiter, ratio, growth, whitecap,
+                    own_idxp, spectrum,
                 )
                 kept.append(held)
+                sent = sent[0] if sent else first
                 received.append(lax.all_to_all(sent, axes, split_axis=0, concat_axis=0, tiled=True))
-            slot = deck[:, 0] // RUN
-            off = offs[:, 0]
+            idxu, idxp, off, slot = tables(runs, row_runs, deck, wet)
+            off, slot = off.reshape(total), slot.reshape(total)
             wet_runs = wet.reshape(total, RUN)
             returned = []
             for chunk in range(chunks):

time: 356 us -> 337 us (0.947)
  local copies, waits for them, and re-layouts: 31.3 us -> 8.91 us
  Pallas kernels: 114 us -> 120 us
  waiting for transfers between devices: 186 us -> 182 us
    all_to_all x1 -> x0, waiting for transfers between devices: 65.2 us -> none  [run(): lax.all_to_all(first.reshape(devices, cap, SUB, RUN), axes, split_axis=0,...]
    all_to_all x1 -> x2, waiting for transfers between devices: 23.9 us -> 88.4 us  [run(): lax.all_to_all(sent, axes, split_axis=0, concat_axis=0, tiled=True)]
    cond x32 -> x2, local copies, waits for them, and re-layouts: 20.1 us -> 0.01 us
    pallas_call x1, Pallas kernels: 20.9 us -> 10.5 us  [begin(): pl.pallas_call(body, in_specs=[smem, vmem, vmem, vmem, vmem, vmem, vmem,...]
    all_to_all x1 -> x2, starting transfers between devices: 4.12 us -> 11.6 us  [run(): lax.all_to_all(sent, axes, split_axis=0, concat_axis=0, tiled=True)]
    all_to_all x1 -> x0, starting transfers between devices: 7.3 us -> none  [run(): lax.all_to_all(first.reshape(devices, cap, SUB, RUN), axes, split_axis=0,...]
    pallas_call x1 -> x2, Pallas kernels: 5.25 us -> 12 us  [sources(): pl.pallas_call(body, grid=(steps,), in_specs=[pl.BlockSpec(memory_space=p...]
    pallas_call x2, Pallas kernels: 70 us -> 75.5 us  [propagate(): pl.pallas_call(body, in_specs=[smem] * 3 + [vmem] * 7, out_specs=vmem, ou...]
  transfers between devices with their start and end apart: 4 -> 4, of which waited for: 4 -> 4; matrix products, arithmetic and copies ran while one was open for 4% -> 3% of each run, Pallas kernels for 24% -> 31%
where the time goes in v2:
time: 337 us
  waiting for transfers between devices  182 us (54%)
  Pallas kernels  120 us (36%)
  starting transfers between devices  19.6 us (6%)
  local copies, waits for them, and re-layouts  8.91 us (3%)
  other arithmetic  4.08 us (1%)
    all_to_all x2, waiting for transfers between devices, run(): lax.all_to_all(sent.reshape(devices, cap, SUB, RUN), axes, split_axis=0,...  93.8 us
    all_to_all x2, waiting for transfers between devices, run(): lax.all_to_all(sent, axes, split_axis=0, concat_axis=0, tiled=True)  88.4 us
    pallas_call x2, Pallas kernels, propagate(): pl.pallas_call(body, in_specs=[smem] * 3 + [vmem] * 7, out_specs=vmem, ou...  75.5 us
    pallas_call x2, Pallas kernels, finish(): pl.pallas_call(body, grid=(1,), in_specs=specs, out_specs=[far, whole(SUB...  13.5 us
    pallas_call x2, Pallas kernels, sources(): pl.pallas_call(body, grid=(steps,), in_specs=[pl.BlockSpec(memory_space=p...  12 us
    all_to_all x2, starting transfers between devices, run(): lax.all_to_all(sent, axes, split_axis=0, concat_axis=0, tiled=True)  11.6 us
    pallas_call x1, Pallas kernels, begin(): pl.pallas_call(body, in_specs=[smem, vmem, vmem, vmem, vmem, vmem, vmem,...  10.5 us
    pallas_call x1, Pallas kernels, tables(): pl.pallas_call(body, in_specs=[vmem, vmem], out_specs=[vmem] * 4, out_sha...  8.86 us
  transfers between devices with their start and end apart: 4, of which 4 were waited for; matrix products, arithmetic and copies ran while one was open for 3% of the time, Pallas kernels for 31%

profile of v2, /device:TPU:0, one launch (start us, length us, event | category | flops | bytes accessed | tf_op | source)
XLA Modules:
  0.0 336.8 jit_solution(2188177100087583843)
XLA Ops:
  0.7 10.5 %begin.1 = (f32[32,25,8,128]{3,2,1,0:T(8,128)}, f32[32,32,8,128]{3,2,1,0:T(8,128)}, s32[32,128]{1,0:T(8,128)S(1)}, s32[32,128]{1,0:T(8,128)S(1)}, s32[32,128]{1,...) custom-call(s32[1]{0:T(128)} %bitcast.30.refs_0_, s32[1024,128]{1,0:T(8,128)} %bitcast.57, s32[256,512]{1,0:T(8,128)} %refs_2_.1, ...), custom_call_target="tpu_custom_call" | custom-call | flops 20971520 | bytes 20971520 | tf_op jit(solution)/shard_map/begin/pallas_call | solution.py:330
  12.0 324.8 %conditional.1 = (f32[512,4096]{1,0:T(8,128)}, f32[4096]{0:T(1024)}) conditional(s32[]{:T(128)} %bitcast.36, (s32[1024,128]{1,0:T(8,128)S(1)}, s32[256,512]{1,0:T(8,128)S(1)}, s32[]{:T(128)}, f32[16]{0:T(128)S(1)}, s32[512]{0:T(512)S(1)}, /*index=5*/f32[512]{0:T(512)S(1)}, f32[512]{0:T(512)S(1)}, s32[32,128]{1,0:T(8,128)S(1)}, ...), branch_computations={%region_0.3_spmd, %region_3.6_spmd} | conditional | flops 507515520 | bytes 189867600 | solution.py:775
  12.0 7.6 %all-to-all-start.6 = ((f32[32,25,8,128]{3,2,1,0:T(8,128)}), f32[32,25,8,128]{3,2,1,0:T(8,128)}, u32[]{:S(2)}, u32[]{:S(2)}) async-start(f32[32,25,8,128]{3,2,1,0:T(8,128)} %get-tuple-element.105), calls=%async_computation.6 | async-start | bytes 6553600 | tf_op jit(solution)/shard_map/cond/branch_1_fun/all_to_all | solution.py:739
  19.6 7.1 %sources.6 = (f32[256,4096]{1,0:T(8,128)}, f32[32,25,8,128]{3,2,1,0:T(8,128)}) custom-call(s32[32,128]{1,0:T(8,128)S(1)} %get-tuple-element.85.refs_0_, f32[1,4096]{1,0:T(1,128)S(1)} %get-tuple-element.94.refs_1_, s32[1,4096]{1,0:T(1,128)S(1)} %get-tuple-element.95.refs_2_, f32[8,4096]{1,0:T(8,128)S(1)} %get-tuple-element.96.refs_3_, ...), custom_call_target="tpu_custom_call" | custom-call | flops 10485760 | bytes 12582912 | tf_op jit(solution)/shard_map/cond/branch_1_fun/sources/pallas_call | solution.py:442
  26.7 67.1 %all-to-all-done.6 = f32[32,25,8,128]{3,2,1,0:T(8,128)} async-done(((f32[32,25,8,128]{3,2,1,0:T(8,128)}), f32[32,25,8,128]{3,2,1,0:T(8,128)}, u32[]{:S(2)}, u32[]{:S(2)}) %all-to-all-start.6) | async-done | bytes 3276832 | tf_op jit(solution)/shard_map/cond/branch_1_fun/all_to_all | solution.py:739
  93.7 4.0 %all-to-all-start.4 = ((f32[32,25,8,128]{3,2,1,0:T(8,128)}), f32[32,25,8,128]{3,2,1,0:T(8,128)}, u32[]{:S(2)}, u32[]{:S(2)}) async-start(f32[32,25,8,128]{3,2,1,0:T(8,128)} %get-tuple-element.101), calls=%async_computation.4 | async-start | bytes 6553600 | tf_op jit(solution)/shard_map/cond/branch_1_fun/all_to_all | solution.py:739
  97.7 0.6 gather_fusion.6
  98.5 0.8 reshape.488.refs_6_
  99.4 0.6 gather_fusion.7
  100.0 0.7 reduce_max.35
  100.7 8.9 %tables.3 = (s32[1024,128]{1,0:T(8,128)}, s32[1024,128]{1,0:T(8,128)}, s32[8,128]{1,0:T(8,128)}, s32[8,128]{1,0:T(8,128)}) custom-call(s32[1024,128]{1,0:T(8,128)S(1)} %get-tuple-element.87.refs_0_, s32[256,512]{1,0:T(8,128)S(1)} %get-tuple-element.88.refs_1_), custom_call_target="tpu_custom_call" | custom-call | flops 268435456 | bytes 2097152 | tf_op jit(solution)/shard_map/cond/branch_1_fun/tables/pallas_call | solution.py:389
  109.6 1.3 pad_add_fusion.3.refs_2_
  110.9 0.7 broadcast_in_dim.17.refs_9_
  111.6 0.7 broadcast_in_dim.15.refs_7_
  112.2 0.7 broadcast_in_dim.16.refs_8_
  112.9 37.8 %propagate.7 = f32[800,8,128]{2,1,0:T(8,128)} custom-call(s32[1024]{0:T(1024)} %bitcast.82, s32[1024]{0:T(1024)} %bitcast.80, s32[3]{0:T(128)} %pad_add_fusion.3.refs_2_, f32[800,8,128]{2,1,0:T(8,128)} %bitcast.27.refs_3_, s32[1024,128]{1,0:T(8,128)} %get-tuple-element.102.refs_4_, s32[1024,128]{1,0:T(8,128)} %get-tuple-element.103.refs_5_, ...), custom_call_target="tpu_custom_call" | custom-call | flops 104857600 | bytes 41943040 | tf_op jit(solution)/shard_map/cond/branch_1_fun/propagate/pallas_call | solution.py:582
  150.6 21.3 %all-to-all-done.4 = f32[32,25,8,128]{3,2,1,0:T(8,128)} async-done(((f32[32,25,8,128]{3,2,1,0:T(8,128)}), f32[32,25,8,128]{3,2,1,0:T(8,128)}, u32[]{:S(2)}, u32[]{:S(2)}) %all-to-all-start.4) | async-done | bytes 3276832 | tf_op jit(solution)/shard_map/cond/branch_1_fun/all_to_all | solution.py:739
  172.0 3.9 %all-to-all-start.7 = ((f32[32,25,8,128]{3,2,1,0:T(8,128)}), f32[32,25,8,128]{3,2,1,0:T(8,128)S(1)}, u32[]{:S(2)}, u32[]{:S(2)}) async-start(f32[32,25,8,128]{3,2,1,0:T(8,128)} %bitcast.55), calls=%async_computation.7 | async-start | bytes 6553600 | tf_op jit(solution)/shard_map/cond/branch_1_fun/all_to_all | solution.py:761
  176.0 0.6 gather_fusion.5
  177.2 0.6 gather_fusion.4
  178.0 1.3 pad_add_fusion.2.refs_2_
  179.3 0.7 broadcast_in_dim.8.refs_9_
  180.0 0.7 broadcast_in_dim.6.refs_7_
  180.6 0.7 broadcast_in_dim.7.refs_8_
  181.3 37.7 %propagate.6 = f32[800,8,128]{2,1,0:T(8,128)} custom-call(s32[1024]{0:T(1024)} %bitcast.83, s32[1024]{0:T(1024)} %bitcast.81, s32[3]{0:T(128)} %pad_add_fusion.2.refs_2_, f32[800,8,128]{2,1,0:T(8,128)} %bitcast.22.refs_3_, s32[1024,128]{1,0:T(8,128)} %get-tuple-element.102.refs_4_, s32[1024,128]{1,0:T(8,128)} %get-tuple-element.103.refs_5_, ...), custom_call_target="tpu_custom_call" | custom-call | flops 104857600 | bytes 41943040 | tf_op jit(solution)/shard_map/cond/branch_1_fun/propagate/pallas_call | solution.py:582
  219.0 31.2 %all-to-all-done.7.refs_2_ = f32[32,25,8,128]{3,2,1,0:T(8,128)S(1)} async-done(((f32[32,25,8,128]{3,2,1,0:T(8,128)}), f32[32,25,8,128]{3,2,1,0:T(8,128)S(1)}, u32[]{:S(2)}, u32[]{:S(2)}) %all-to-all-start.7) | async-done | bytes 3276832 | tf_op jit(solution)/shard_map/cond/branch_1_fun/all_to_all | solution.py:761
  250.2 4.1 %all-to-all-start.5 = ((f32[32,25,8,128]{3,2,1,0:T(8,128)}), f32[32,25,8,128]{3,2,1,0:T(8,128)}, u32[]{:S(2)}, u32[]{:S(2)}) async-start(f32[32,25,8,128]{3,2,1,0:T(8,128)} %bitcast.56), calls=%async_computation.5 | async-start | bytes 6553600 | tf_op jit(solution)/shard_map/cond/branch_1_fun/all_to_all | solution.py:761
  254.2 4.9 %sources.7.refs_3_ = f32[256,4096]{1,0:T(8,128)} custom-call(s32[32,128]{1,0:T(8,128)S(1)} %get-tuple-element.85.refs_0_, f32[1,4096]{1,0:T(1,128)S(1)} %get-tuple-element.94.refs_1_, s32[1,4096]{1,0:T(1,128)S(1)} %get-tuple-element.95.refs_2_, f32[8,4096]{1,0:T(8,128)S(1)} %get-tuple-element.96.refs_3_, f32[4,1,128]{2,1,0:T(1,128)S(1)} %bitcast.70, ...), custom_call_target="tpu_custom_call" | custom-call | flops 10485760 | bytes 12582912 | tf_op jit(solution)/shard_map/cond/branch_1_fun/sources/pallas_call | solution.py:442
  259.2 6.7 %finish.6 = (f32[512,4096]{1,0:T(8,128)}, f32[8,4096]{1,0:T(8,128)}) custom-call(s32[32,128]{1,0:T(8,128)S(1)} %get-tuple-element.85.refs_0_, s32[32,128]{1,0:T(8,128)S(1)} %get-tuple-element.86.refs_1_, f32[32,25,8,128]{3,2,1,0:T(8,128)} %copy-done.2, f32[256,4096]{1,0:T(8,128)} %sources.7.refs_3_), custom_call_target="tpu_custom_call" | custom-call | flops 4194304 | bytes 12582912 | tf_op jit(solution)/shard_map/cond/branch_1_fun/finish/pallas_call | solution.py:683
  265.9 62.6 %all-to-all-done.5.refs_2_ = f32[32,25,8,128]{3,2,1,0:T(8,128)} async-done(((f32[32,25,8,128]{3,2,1,0:T(8,128)}), f32[32,25,8,128]{3,2,1,0:T(8,128)}, u32[]{:S(2)}, u32[]{:S(2)}) %all-to-all-start.5) | async-done | bytes 3276832 | tf_op jit(solution)/shard_map/cond/branch_1_fun/all_to_all | solution.py:761
  328.5 6.8 %finish.7 = (f32[512,4096]{1,0:T(8,128)}, f32[8,4096]{1,0:T(8,128)}) custom-call(s32[32,128]{1,0:T(8,128)S(1)} %get-tuple-element.85.refs_0_, s32[32,128]{1,0:T(8,128)S(1)} %get-tuple-element.86.refs_1_, f32[32,25,8,128]{3,2,1,0:T(8,128)} %all-to-all-done.5.refs_2_, f32[256,4096]{1,0:T(8,128)} %get-tuple-element.104.refs_3_, ...), custom_call_target="tpu_custom_call", output_to_operand_aliasing={{0}: (5, {})} | custom-call | flops 4194304 | bytes 12582912 | tf_op jit(solution)/shard_map/cond/branch_1_fun/finish/pallas_call | solution.py:683
  335.3 1.5 slice.29
  (27 shorter events, 0.8 us)
Async XLA Ops:
  0.6 11.2 %copy-start = (f32[16]{0:T(128)S(1)}, f32[16]{0:T(128)}, u32[]{:S(2)}) copy-start(f32[16]{0:T(128)} %param.15) | copy-start | bytes 196
  0.6 11.2 %copy-start.1 = (s32[512]{0:T(512)S(1)}, s32[512]{0:T(512)}, u32[]{:S(2)}) copy-start(s32[512]{0:T(512)} %param.16) | copy-start | bytes 6148
  0.7 11.2 %copy-start.3 = (s32[256,512]{1,0:T(8,128)S(1)}, s32[256,512]{1,0:T(8,128)}, u32[]{:S(2)}) copy-start(s32[256,512]{1,0:T(8,128)} %refs_2_.1) | copy-start | bytes 1572868
  0.7 11.2 %copy-start.4 = (s32[131072]{0:T(1024)S(1)}, s32[131072]{0:T(1024)}, u32[]{:S(2)}) copy-start(s32[131072]{0:T(1024)} %param.18) | copy-start | bytes 1572868
  0.7 11.2 %copy-start.5 = (f32[4096]{0:T(1024)S(1)}, f32[4096]{0:T(1024)}, u32[]{:S(2)}) copy-start(f32[4096]{0:T(1024)} %param.12) | copy-start | bytes 49156
  0.7 11.2 %copy-start.6 = (s32[4096]{0:T(1024)S(1)}, s32[4096]{0:T(1024)}, u32[]{:S(2)}) copy-start(s32[4096]{0:T(1024)} %param.17) | copy-start | bytes 49156
  0.7 11.2 %copy-start.7 = (f32[512]{0:T(512)S(1)}, f32[512]{0:T(512)}, u32[]{:S(2)}) copy-start(f32[512]{0:T(512)} %param.13) | copy-start | bytes 6148
  0.7 11.2 %copy-start.8 = (f32[512]{0:T(512)S(1)}, f32[512]{0:T(512)}, u32[]{:S(2)}) copy-start(f32[512]{0:T(512)} %param.14) | copy-start | bytes 6148
  12.0 81.8 %all-to-all-start.6 = ((f32[32,25,8,128]{3,2,1,0:T(8,128)}), f32[32,25,8,128]{3,2,1,0:T(8,128)}, u32[]{:S(2)}, u32[]{:S(2)}) async-start(f32[32,25,8,128]{3,2,1,0:T(8,128)} %get-tuple-element.105), calls=%async_computation.6 | async-start | bytes 6553600 | tf_op jit(solution)/shard_map/cond/branch_1_fun/all_to_all | solution.py:739
  93.7 78.2 %all-to-all-start.4 = ((f32[32,25,8,128]{3,2,1,0:T(8,128)}), f32[32,25,8,128]{3,2,1,0:T(8,128)}, u32[]{:S(2)}, u32[]{:S(2)}) async-start(f32[32,25,8,128]{3,2,1,0:T(8,128)} %get-tuple-element.101), calls=%async_computation.4 | async-start | bytes 6553600 | tf_op jit(solution)/shard_map/cond/branch_1_fun/all_to_all | solution.py:739
  172.0 78.2 %all-to-all-start.7 = ((f32[32,25,8,128]{3,2,1,0:T(8,128)}), f32[32,25,8,128]{3,2,1,0:T(8,128)S(1)}, u32[]{:S(2)}, u32[]{:S(2)}) async-start(f32[32,25,8,128]{3,2,1,0:T(8,128)} %bitcast.55), calls=%async_computation.7 | async-start | bytes 6553600 | tf_op jit(solution)/shard_map/cond/branch_1_fun/all_to_all | solution.py:761
  250.2 9.0 %copy-start.2 = (f32[32,25,8,128]{3,2,1,0:T(8,128)}, f32[32,25,8,128]{3,2,1,0:T(8,128)S(1)}, u32[]{:S(2)}) copy-start(f32[32,25,8,128]{3,2,1,0:T(8,128)S(1)} %all-to-all-done.7.refs_2_) | copy-start | bytes 9830404 | tf_op jit(solution)/shard_map/cond
  250.2 78.3 %all-to-all-start.5 = ((f32[32,25,8,128]{3,2,1,0:T(8,128)}), f32[32,25,8,128]{3,2,1,0:T(8,128)}, u32[]{:S(2)}, u32[]{:S(2)}) async-start(f32[32,25,8,128]{3,2,1,0:T(8,128)} %bitcast.56), calls=%async_computation.5 | async-start | bytes 6553600 | tf_op jit(solution)/shard_map/cond/branch_1_fun/all_to_all | solution.py:761

commit v3 on v2

--- a/solution.py
+++ b/solution.py
@@ -8,6 +8,7 @@
 from jax.sharding import PartitionSpec as P
 
 DIRS = 32
+QUADRANTS = 4
 MAXSUB = 8
 RUN = 128
 SUB = 8
@@ -15,8 +16,9 @@
 rate_limit = 0.5
 time_step = 0.5
 
-FINISH_PARTS = 8
-VMEM_GRANT = 60 * 1024 * 1024
+FLOWS, FLOWS_AND_STAYS, STAYS, DRY = range(4)
+
+VMEM_GRANT = 62 * 1024 * 1024
 
 
 def plain_sources(spectrum, wind, growth, whitecap, limiter):
@@ -119,9 +121,18 @@
     return jnp.broadcast_to(block[j : j + 1, :], (SUB, RUN))
 
 
+def split(off):
+    first = lax.shift_right_logical(off, RUN.bit_length() - 1)
+    return first, off - first * RUN
+
+
 def place(off, cap):
-    first = jnp.minimum(off // RUN, cap - 1)
+    first = jnp.minimum(split(off)[0], cap - 1)
     return first, off - first * RUN
+
+
+def place_all(off, q, runs, cap):
+    return [place(off[q * runs + t, 0], cap) for t in range(runs)]
 
 
 def columns(t):
@@ -157,14 +168,29 @@
     return jnp.where(mask, 1.0, 0.0).astype(jnp.bfloat16)
 
 
-def lay_out(wet, sea, row_runs):
-    halves = wet.shape[0] // RUN
+def neighbours(wet):
+    rows, cols = wet.shape
+    row = lax.broadcasted_iota(jnp.int32, wet.shape, 0)
+    north = jnp.where(row < rows - 1, pltpu.roll(wet, rows - 1, 0), 0.0)
+    south = jnp.where(row > 0, pltpu.roll(wet, 1, 0), 0.0)
+    return north, south, pltpu.roll(wet, cols - 1, 1), pltpu.roll(wet, 1, 1)
+
+
+def flowing(wet):
+    north, south, east, west = neighbours(wet)
+    return [
+        wet * jnp.maximum(along, across)
+        for along, across in ((north, east), (north, west), (south, west), (south, east))
+    ]
+
+
+def lay_out(mask, sea, column, row_runs):
+    halves = mask.shape[0] // RUN
+    mask = mask.astype(jnp.bfloat16)
     for q in range(row_runs):
         for h in range(halves):
             k = q * halves + h
-            sea[k * RUN : (k + 1) * RUN, :] = wet[h * RUN : (h + 1) * RUN, columns(q)].astype(
-                jnp.float32
-            ).astype(jnp.bfloat16)
+            sea[k * RUN : (k + 1) * RUN, columns(column)] = mask[h * RUN : (h + 1) * RUN, columns(q)]
 
 
 def picks(slot, row_runs, halves):
@@ -179,7 +205,7 @@
     )
 
 
-def stream_tables(wet_here, before):
+def stream_tables(wet_here, before, inverse=True):
     lane = lanes(wet_here.shape[0])
     wet_low = wet_here.astype(jnp.bfloat16)
     square = lambda: (lax.broadcasted_iota(jnp.int32, (RUN, RUN), 0), lanes(RUN))
@@ -192,7 +218,7 @@
     idxu = jnp.where(wet_here > 0.5, spot, spot + RUN)
     nth = jnp.bitwise_and(lane - off, RUN - 1)
     at = jnp.zeros(nth.shape, jnp.int32)
-    bit = RUN // 2
+    bit = RUN // 2 if inverse else 0
     while bit:
         probe = lane_gather(through, at + (bit - 1))
         at = jnp.where(probe <= nth, at + bit, at)
@@ -202,12 +228,12 @@
 
 def begin_kernel(
     small, runs, row_runs, rank, deck, wet, wind, limiter, growth, whitecap, spectrum,
-    sent_small, sent_full, own_idxu, own_idxp, own_off, ratio, need,
+    sent_small, sent_full, own_code, own_idxp, own_off, ratio, need,
     values, packed, sea, total, grown, capped, off, in_sems, sent_sems, off_sem,
 ):
     comps = values.shape[0]
     slots = deck.shape[0]
-    groups = packed.shape[0]
+    groups = packed.shape[1] * QUADRANTS
     parts = in_sems.shape[0]
     part = comps // parts
 
@@ -219,22 +245,36 @@
         fetch(p).start()
 
     halves = wet.shape[0] // RUN
-    lay_out(wet, sea, row_runs)
-    ones = jnp.ones((RUN, RUN), jnp.bfloat16)
+    wet_f = wet[...].astype(jnp.float32)
+    for k, mask in enumerate(flowing(wet_f) + [wet_f]):
+        lay_out(mask, sea, k, row_runs)
 
     mine = pl.ds(pl.multiple_of(rank[0] * runs, SUB), runs)
-    wet_mine = dot(picks(deck[mine, :] // RUN, row_runs, halves), sea[...])
-    below = lax.broadcasted_iota(jnp.int32, (runs, runs), 1) < lax.broadcasted_iota(jnp.int32, (runs, runs), 0)
-    own_off[...], own_idxu[...], own_idxp[...] = stream_tables(wet_mine, one(below))
+    found = dot(picks(deck[mine, :] // RUN, row_runs, halves), sea[...])
+    lane = lanes(RUN)
+    row = lax.broadcasted_iota(jnp.int32, (RUN, RUN), 0)
+    same = lane // runs == row // runs
+    masks = jnp.concatenate([found[:, columns(q)] for q in range(QUADRANTS)], axis=0)
+    own_off[...], idxu, own_idxp[...] = stream_tables(masks, one(same & (lane < row)))
+    land = found[:, columns(QUADRANTS)] < 0.5
+    for q in range(QUADRANTS):
+        near = slice(q * runs, (q + 1) * runs)
+        back = (q + 2) % QUADRANTS
+        there = idxu[back * runs : (back + 1) * runs, :]
+        comes = there < RUN
+        goes = idxu[near, :] < RUN
+        kind = jnp.where(comes, jnp.where(goes, FLOWS, FLOWS_AND_STAYS), jnp.where(land, DRY, STAYS))
+        own_code[near, :] = jnp.bitwise_and(there, RUN - 1) + RUN * kind
     off_copy = pltpu.make_async_copy(own_off, off, off_sem)
     off_copy.start()
 
-    same = one(lanes(RUN) // runs == lax.broadcasted_iota(jnp.int32, (RUN, RUN), 0) // runs)
-    counts = dot(sea[...], ones).astype(jnp.bfloat16)
+    wide = (QUADRANTS * RUN, RUN)
+    which = lax.broadcasted_iota(jnp.int32, wide, 0) // RUN == lanes(wide[0]) // (RUN // QUADRANTS)
+    counts = dot(sea[:, : QUADRANTS * RUN], one(which)).astype(jnp.bfloat16)
     most = None
     for b in range(slots // RUN):
         here = dot(picks(deck[b * RUN : (b + 1) * RUN, :] // RUN, row_runs, halves), counts)
-        sums = dot(same, here.astype(jnp.bfloat16))
+        sums = dot(one(same), here.astype(jnp.bfloat16))
         most = sums if most is None else jnp.maximum(most, sums)
     most = jnp.max(most).astype(jnp.int32)
     need[0] = most
@@ -257,59 +297,57 @@
 
     off_copy.wait()
     fits_small = most <= small * RUN
-    cap = jnp.where(fits_small, small, runs)
     reg_lane = lanes()
-    several = 8
-    tall = several * SUB
-
-    def pass_on(i, size, target):
-        these = pl.ds(i * several, several)
-        return pltpu.make_async_copy(packed.at[these, pl.ds(0, size)], target.at[these], sent_sems.at[i])
-
-    def some(i, carry):
-        spots = [place(off[t, 0], cap) for t in range(runs)]
-        here = packed.at[pl.ds(i * several, several)]
-        for g in range(several):
-            rows = pl.ds(pl.multiple_of(i * tall + g * SUB, SUB), SUB)
-            forced = []
-            for t in range(runs):
-                cols = columns(t)
-                wind_t = jnp.broadcast_to(wind[:, cols], (SUB, RUN))
-                limited = jnp.broadcast_to(limiter[:, cols], (SUB, RUN)) == 1
-                forced.append(
-                    force(values[rows, cols], wind_t, ratio[:, cols], limited, grown[rows, :], capped[rows, :])
-                )
-            sent = [lane_gather(forced[t], rows_of(own_idxp, t)) for t in range(runs)]
-
-            def store(at, value, g=g):
-                here[g, at] = value
-
-            write_stream(sent, spots, reg_lane, store, cap)
+    per = groups // QUADRANTS
+
+    def pass_on(q, size, target):
+        return pltpu.make_async_copy(packed.at[q, :, pl.ds(0, size)], target.at[:, q], sent_sems.at[q])
+
+    for q in range(QUADRANTS):
+        index = [slice(g * SUB, (g + 1) * SUB) for g in range(q, groups, QUADRANTS)]
+        stream = packed.at[q]
+        merged, last = [None] * per, [None] * per
+        first_before = None
+        for t in range(runs):
+            cols = columns(t)
+            wind_t = jnp.broadcast_to(wind[:, cols], (SUB, RUN))
+            limited = jnp.broadcast_to(limiter[:, cols], (SUB, RUN)) == 1
+            ratio_t = ratio[:, cols]
+            picked = rows_of(own_idxp, q * runs + t)
+            offset = off[q * runs + t, 0]
+            first, start = split(offset)
+            taken = reg_lane >= start
+            for m, rows in enumerate(index):
+                value = force(values[rows, cols], wind_t, ratio_t, limited, grown[rows, :], capped[rows, :])
+                value = lane_gather(value, picked)
+                if t == 0:
+                    merged[m] = value
+                else:
+                    before = jnp.where(first == first_before, merged[m], last[m])
+                    merged[m] = jnp.where(taken, value, before)
+                last[m] = value
+                if t == runs - 1:
+                    stream[m, first + 1] = value
+                stream[m, first] = merged[m]
+            first_before = first
 
         @pl.when(fits_small)
-        def _():
-            pass_on(i, small, sent_small).start()
+        def _(q=q):
+            pass_on(q, small, sent_small).start()
 
         @pl.when(jnp.logical_not(fits_small))
-        def _():
-            pass_on(i, runs, sent_full).start()
-
-        return carry
-
-    lax.fori_loop(0, groups // several, some, 0)
-
-    def drain(i, carry):
+        def _(q=q):
+            pass_on(q, runs, sent_full).start()
+
+    for q in range(QUADRANTS):
+
         @pl.when(fits_small)
-        def _():
-            pass_on(i, small, sent_small).wait()
+        def _(q=q):
+            pass_on(q, small, sent_small).wait()
 
         @pl.when(jnp.logical_not(fits_small))
-        def _():
-            pass_on(i, runs, sent_full).wait()
-
-        return carry
-
-    lax.fori_loop(0, groups // several, drain, 0)
+        def _(q=q):
+            pass_on(q, runs, sent_full).wait()
 
 
 def begin(small, runs, row_runs, groups, rank, deck, wet, wind, limiter, growth, whitecap, spectrum):
@@ -332,24 +370,24 @@
         in_specs=[smem, vmem, vmem, vmem, vmem, vmem, vmem, far],
         out_specs=[far] * 2 + [vmem] * 4 + [smem],
         out_shape=[
-            f32(groups, small, SUB, RUN),
-            f32(groups, runs, SUB, RUN),
-            i32(runs, RUN),
-            i32(runs, RUN),
-            i32(runs, RUN),
+            f32(groups // QUADRANTS, QUADRANTS, small, SUB, RUN),
+            f32(groups // QUADRANTS, QUADRANTS, runs, SUB, RUN),
+            i32(QUADRANTS * runs, RUN),
+            i32(QUADRANTS * runs, RUN),
+            i32(QUADRANTS * runs, RUN),
             f32(SUB, points),
             i32(1),
         ],
         scratch_shapes=[
             pltpu.VMEM((comps, points), jnp.float32),
-            pltpu.VMEM((groups, runs, SUB, RUN), jnp.float32),
-            pltpu.VMEM((slots, RUN), jnp.bfloat16),
+            pltpu.VMEM((QUADRANTS, groups // QUADRANTS, runs + 1, SUB, RUN), jnp.float32),
+            pltpu.VMEM((slots, (QUADRANTS + 1) * RUN), jnp.bfloat16),
             pltpu.VMEM((SUB, points), jnp.float32),
             pltpu.VMEM((block, RUN), jnp.float32),
             pltpu.VMEM((block, RUN), jnp.float32),
-            pltpu.SMEM((runs, RUN), jnp.int32),
+            pltpu.SMEM((QUADRANTS * runs, RUN), jnp.int32),
             pltpu.SemaphoreType.DMA((parts,)),
-            pltpu.SemaphoreType.DMA((groups,)),
+            pltpu.SemaphoreType.DMA((QUADRANTS,)),
             pltpu.SemaphoreType.DMA,
         ],
         cost_estimate=pl.CostEstimate(flops=10 * cells, bytes_accessed=10 * cells, transcendentals=cells),
@@ -358,8 +396,14 @@
     )(rank, deck, wet, wind, limiter, growth, whitecap, spectrum)
 
 
-def tables_kernel(runs, row_runs, deck, wet, idxu, idxp, off, slot, sea):
-    lay_out(wet, sea, row_runs)
+def tables_kernel(runs, row_runs, info, deck, wet, idxu, idxp, off_in, off_out, slot, sea):
+    wet_f = wet[...].astype(jnp.float32)
+    north, south, east, west = neighbours(wet_f)
+    from_south, from_west = info[0] < 0, info[1] > 0
+    ahead = jnp.maximum(jnp.where(from_south, north, south), jnp.where(from_west, east, west))
+    behind = jnp.maximum(jnp.where(from_south, south, north), jnp.where(from_west, west, east))
+    lay_out(wet_f * ahead, sea, 0, row_runs)
+    lay_out(wet_f * behind, sea, 1, row_runs)
     row = lax.broadcasted_iota(jnp.int32, (RUN, RUN), 0)
     lane = lanes(RUN)
     before = one((lane < row) & (lane // runs == row // runs))
@@ -368,18 +412,20 @@
     def block(b, carry):
         here = pl.ds(pl.multiple_of(b * RUN, RUN), RUN)
         slot_b = deck[here, :] // RUN
-        off_b, idxu[here, :], idxp[here, :] = stream_tables(
-            dot(picks(slot_b, row_runs, halves), sea[...]), before
-        )
-        off[pl.ds(b, 1), :] = jnp.transpose(off_b)[:1, :]
+        found = dot(picks(slot_b, row_runs, halves), sea[...])
+        off_b, idxu[here, :], _ = stream_tables(found[:, columns(0)], before, False)
+        off_in[pl.ds(b, 1), :] = jnp.transpose(off_b)[:1, :]
+        off_b, _, idxp[here, :] = stream_tables(found[:, columns(1)], before)
+        off_out[pl.ds(b, 1), :] = jnp.transpose(off_b)[:1, :]
         slot[pl.ds(b, 1), :] = jnp.transpose(slot_b)[:1, :]
         return carry
 
     lax.fori_loop(0, deck.shape[0] // RUN, block, 0)
 
 
-def tables(runs, row_runs, deck, wet):
+def tables(runs, row_runs, info, deck, wet):
     slots = deck.shape[0]
+    smem = pl.BlockSpec(memory_space=pltpu.SMEM)
     vmem = pl.BlockSpec(memory_space=pltpu.VMEM)
     i32 = lambda *shape: jax.ShapeDtypeStruct(shape, jnp.int32)
 
@@ -388,24 +434,25 @@
 
     return pl.pallas_call(
         body,
-        in_specs=[vmem, vmem],
-        out_specs=[vmem] * 4,
-        out_shape=[i32(slots, RUN), i32(slots, RUN), i32(slots // RUN, RUN), i32(slots // RUN, RUN)],
-        scratch_shapes=[pltpu.VMEM((slots, RUN), jnp.bfloat16)],
-        cost_estimate=pl.CostEstimate(flops=2 * slots * slots * RUN, bytes_accessed=16 * slots * RUN, transcendentals=0),
+        in_specs=[smem, vmem, vmem],
+        out_specs=[vmem] * 5,
+        out_shape=[i32(slots, RUN)] * 2 + [i32(slots // RUN, RUN)] * 3,
+        scratch_shapes=[pltpu.VMEM((slots, 2 * RUN), jnp.bfloat16)],
+        cost_estimate=pl.CostEstimate(flops=4 * slots * slots * RUN, bytes_accessed=16 * slots * RUN, transcendentals=0),
         compiler_params=pltpu.CompilerParams(vmem_limit_bytes=VMEM_GRANT),
         name="tables",
-    )(deck, wet)
-
-
-def source_kernel(cap, runs, off, wind, limiter, ratio, growth, whitecap, idxp, spectrum, forced, *packed):
+    )(info, deck, wet)
+
+
+def source_kernel(cap, runs, off, wind, limiter, ratio, growth, whitecap, idxp, code, decay, spectrum, held, *packed):
     groups = spectrum.shape[0] // SUB
     lane = lanes()
     block = groups * SUB
     grown = spread(growth[...].reshape(1, RUN))
     capped = spread(whitecap[...].reshape(1, RUN))
-    spots = [place(off[t, 0], cap) for t in range(runs)]
+    spots = [place_all(off, q, runs, cap) for q in range(QUADRANTS)]
     for g in range(groups):
+        q = g % QUADRANTS
         rows = slice(g * SUB, (g + 1) * SUB)
         values = []
         for t in range(runs):
@@ -416,17 +463,20 @@
                 force(spectrum[rows, cols], wind_t, ratio[:, cols], limited, grown[rows, :], capped[rows, :])
             )
         for t in range(runs):
-            forced[rows, columns(t)] = values[t]
+            mark = rows_of(code, q * runs + t)
+            kept = jnp.where(mark < DRY * RUN, decay[rows, :], 1.0)
+            kept = jnp.where(mark < FLOWS_AND_STAYS * RUN, 0.0, kept)
+            held[rows, columns(t)] = kept * values[t]
         if packed:
-            sent = [lane_gather(values[t], rows_of(idxp, t)) for t in range(runs)]
+            sent = [lane_gather(values[t], rows_of(idxp, q * runs + t)) for t in range(runs)]
 
             def store(at, value, g=g):
                 packed[0][g, at] = value
 
-            write_stream(sent, spots, lane, store, cap)
-
-
-def sources(cap, chunk, groups, pack, off, wind, limiter, ratio, growth, whitecap, idxp, spectrum):
+            write_stream(sent, spots[q], lane, store, cap)
+
+
+def sources(cap, chunk, groups, pack, off, wind, limiter, ratio, growth, whitecap, idxp, code, decay, spectrum):
     points = spectrum.shape[1]
     runs = points // RUN
     block = RUN
@@ -449,7 +499,9 @@
             pl.BlockSpec((SUB, points), whole),
             pl.BlockSpec((1, 1, RUN), lambda i: (base + i, 0, 0)),
             pl.BlockSpec((1, 1, RUN), lambda i: (base + i, 0, 0)),
-            pl.BlockSpec((runs, RUN), whole),
+            pl.BlockSpec((QUADRANTS * runs, RUN), whole),
+            pl.BlockSpec((QUADRANTS * runs, RUN), whole),
+            pl.BlockSpec((block, RUN), lambda i: (base + i, 0)),
             pl.BlockSpec((block, points), lambda i: (base + i, 0)),
         ],
         out_specs=[
@@ -463,11 +515,11 @@
         cost_estimate=pl.CostEstimate(flops=10 * cells, bytes_accessed=12 * cells, transcendentals=2 * cells),
         compiler_params=pltpu.CompilerParams(vmem_limit_bytes=VMEM_GRANT),
         name="sources",
-    )(off, wind, limiter, ratio, growth[:, None, :], whitecap[:, None, :], idxp, spectrum)
+    )(off, wind, limiter, ratio, growth[:, None, :], whitecap[:, None, :], idxp, code, decay, spectrum)
 
 
 def propagate_kernel(
-    cap, runs, row_runs, slot, off, info, recv, idxu, idxp, wet, cx, cy, counts, sent, field, other, wide
+    cap, runs, row_runs, slot, off_in, off_out, info, recv, idxu, idxp, wet, cx, cy, counts, sent, field, other, wide
 ):
     total = slot.shape[0]
     lane = lanes()
@@ -494,7 +546,7 @@
         indices = idxu[pl.ds(t0, runs), :]
         done = []
         for j in range(runs):
-            first, start = place(off[t0 + j], cap)
+            first, start = place(off_in[t0 + j], cap)
             second = jnp.minimum(first + 1, cap - 1)
             window = jnp.where(lane >= start, recv[base + first], recv[base + second])
             index = rows_of(indices, j)
@@ -558,7 +610,7 @@
         picked = [
             lane_gather(field[row_runs + slot[t0 + j]], rows_of(indices, j)) for j in range(runs)
         ]
-        spots = [place(off[t0 + j], cap) for j in range(runs)]
+        spots = [place(off_out[t0 + j], cap) for j in range(runs)]
 
         def store(at, value):
             sent[i * cap + at] = value
@@ -569,7 +621,7 @@
     lax.fori_loop(0, total // runs, pack, 0)
 
 
-def propagate(cap, runs, row_runs, slot, off, info, recv, idxu, idxp, wet, cx, cy, counts):
+def propagate(cap, runs, row_runs, slot, off_in, off_out, info, recv, idxu, idxp, wet, cx, cy, counts):
     total = slot.shape[0]
     smem = pl.BlockSpec(memory_space=pltpu.SMEM)
     vmem = pl.BlockSpec(memory_space=pltpu.VMEM)
@@ -581,121 +633,115 @@
     padded = pltpu.VMEM((total + 2 * row_runs, SUB, RUN), jnp.float32)
     return pl.pallas_call(
         body,
-        in_specs=[smem] * 3 + [vmem] * 7,
+        in_specs=[smem] * 4 + [vmem] * 7,
         out_specs=vmem,
         out_shape=jax.ShapeDtypeStruct(recv.shape, jnp.float32),
         scratch_shapes=[padded, padded, pltpu.VMEM((total, SUB, RUN), jnp.float32)],
         cost_estimate=pl.CostEstimate(flops=100 * cells, bytes_accessed=40 * cells, transcendentals=0),
         compiler_params=pltpu.CompilerParams(vmem_limit_bytes=VMEM_GRANT),
         name="propagate",
-    )(slot, off, info, recv, idxu, idxp, wet, cx, cy, counts)
-
-
-def finish_kernel(cap, runs, comps, base, begin, end, off, idxu, recv, forced, *rest):
+    )(slot, off_in, off_out, info, recv, idxu, idxp, wet, cx, cy, counts)
+
+
+def finish_kernel(runs, comps, base, begin, end, off, code, recv, held, *rest):
     if begin:
         out, total, streams, values, stream_sems, value_sems, out_sems = rest
+    elif end:
+        before, _, out, height, streams, values, stream_sems, value_sems, out_sems, total = rest
     else:
         before, _, out, total, streams, values, stream_sems, value_sems, out_sems = rest
     lane = lanes()
-    parts = stream_sems.shape[0]
-    groups = recv.shape[0] // parts
-    tall = groups * SUB
-
-    def arrive(p):
-        some = pl.ds(p * groups, groups)
-        return pltpu.make_async_copy(recv.at[some], streams.at[some], stream_sems.at[p])
-
-    def bring(p):
-        rows = pl.ds(pl.multiple_of(p * tall, SUB), tall)
-        return pltpu.make_async_copy(forced.at[rows], values.at[rows], value_sems.at[p])
-
-    def leave(p):
-        rows = pl.ds(pl.multiple_of(p * tall, SUB), tall)
-        there = pl.ds(pl.multiple_of(base + p * tall, SUB), tall)
-        return pltpu.make_async_copy(values.at[rows], out.at[there], out_sems.at[p])
-
-    for p in range(parts):
-        arrive(p).start()
-        bring(p).start()
+    per, _, cap = recv.shape[:3]
+
+    def arrive(q):
+        return pltpu.make_async_copy(recv.at[:, q], streams.at[q, :, pl.ds(0, cap)], stream_sems.at[q])
+
+    def bring(q):
+        return pltpu.make_async_copy(held.at[:, q], values.at[q], value_sems.at[q])
+
+    def leave(q):
+        return pltpu.make_async_copy(values.at[q], out.at[pl.ds(base, per), q], out_sems.at[q])
+
+    for q in range(QUADRANTS):
+        arrive(q).start()
+        bring(q).start()
     total[...] = jnp.zeros_like(total) if begin else before[...]
-
-    def some(p, carry):
-        arrive(p).wait()
-        bring(p).wait()
-        here = streams.at[pl.ds(p * groups, groups)]
-        block = values.at[pl.ds(pl.multiple_of(p * tall, SUB), tall)]
-        rows = [slice(g * SUB, (g + 1) * SUB) for g in range(groups)]
+    for q in range(QUADRANTS):
+        arrive(q).wait()
+        bring(q).wait()
+        here = streams.at[q]
+        block = values.at[q]
         for t0 in range(0, runs, SUB):
             done = []
             for t in range(t0, t0 + SUB):
-                first, start = place(off[t, 0], cap)
-                second = jnp.minimum(first + 1, cap - 1)
-                index = rows_of(idxu, t)
-                sea = index < RUN
-                index = jnp.bitwise_and(index, RUN - 1)
+                offset = off[(q + 2) % QUADRANTS * runs + t, 0]
+                first, start = split(offset)
+                mark = rows_of(code, q * runs + t)
+                comes = mark < STAYS * RUN
+                index = jnp.bitwise_and(mark, RUN - 1)
                 lower = lane >= start
-                cells = [
-                    lane_gather(jnp.where(lower, here[g, first], here[g, second]), index) for g in range(groups)
-                ]
-                done.append([jnp.where(sea, cells[g], block[rows[g], columns(t)]) for g in range(groups)])
+                settled = []
+                for m in range(per):
+                    window = jnp.where(lower, here[m, first], here[m, first + 1])
+                    cells = jnp.where(comes, lane_gather(window, index), 0.0)
+                    settled.append(cells + block[m, :, columns(t)])
+                done.append(settled)
             for k, settled in enumerate(done):
                 cols = columns(t0 + k)
-                added = total[:, cols]
-                for g in range(groups):
-                    block[rows[g], cols] = settled[g]
-                    added = added + settled[g]
-                total[:, cols] = added
-        leave(p).start()
-        return carry
-
-    lax.fori_loop(0, parts, some, 0)
+                for m in range(per):
+                    block[m, :, cols] = settled[m]
+                while len(settled) > 1:
+                    settled = [sum(settled[n : n + 2]) for n in range(0, len(settled), 2)]
+                total[:, cols] = total[:, cols] + settled[0]
+        leave(q).start()
     if end:
         mean = jnp.sum(total[...], axis=0, keepdims=True) / comps
-        height = 4.0 * jnp.sqrt(mean + 1e-06)
-        total[...] = jnp.broadcast_to(height, total.shape)
-
-    def drain(p, carry):
-        leave(p).wait()
-        return carry
-
-    lax.fori_loop(0, parts, drain, 0)
-
-
-def finish(cap, comps, chunk, begin, end, off, idxu, recv, forced, before, out):
-    block, points = forced.shape
+        mean = 4.0 * jnp.sqrt(mean + 1e-06)
+        for t in range(runs):
+            height[t : t + 1, :] = mean[:, columns(t)]
+    for q in range(QUADRANTS):
+        leave(q).wait()
+
+
+def finish(cap, comps, chunk, begin, end, off, code, recv, held, before, out):
+    block, points = held.shape
     runs = points // RUN
-    parts = FINISH_PARTS
+    per = block // SUB // QUADRANTS
+    recv = recv.reshape(per, QUADRANTS, cap, SUB, RUN)
+    held = held.reshape(per, QUADRANTS, SUB, points)
     smem = pl.BlockSpec(memory_space=pltpu.SMEM)
     whole = lambda *shape: pl.BlockSpec(shape, lambda i: (0, 0))
     far = pl.BlockSpec(memory_space=pltpu.HBM)
-    specs = [smem, whole(runs, RUN), far, far]
-    args = [off, idxu, recv, forced]
+    specs = [smem, whole(QUADRANTS * runs, RUN), far, far]
+    args = [off, code, recv, held]
     aliases = {}
     if not begin:
         specs += [whole(SUB, points), far]
         args += [before, out]
         aliases = {5: 0}
     cells = block * points
+    last = (runs, RUN) if end else (SUB, points)
 
     def body(*refs):
-        finish_kernel(cap, runs, comps, chunk * block, begin, end, *refs)
+        finish_kernel(runs, comps, chunk * per, begin, end, *refs)
 
     return pl.pallas_call(
         body,
         grid=(1,),
         in_specs=specs,
-        out_specs=[far, whole(SUB, points)],
+        out_specs=[far, whole(*last)],
         out_shape=[
-            jax.ShapeDtypeStruct((comps, points), jnp.float32),
-            jax.ShapeDtypeStruct((SUB, points), jnp.float32),
+            jax.ShapeDtypeStruct((comps // SUB // QUADRANTS, QUADRANTS, SUB, points), jnp.float32),
+            jax.ShapeDtypeStruct(last, jnp.float32),
         ],
         scratch_shapes=[
-            pltpu.VMEM(recv.shape, jnp.float32),
-            pltpu.VMEM((block, points), jnp.float32),
-            pltpu.SemaphoreType.DMA((parts,)),
-            pltpu.SemaphoreType.DMA((parts,)),
-            pltpu.SemaphoreType.DMA((parts,)),
-        ],
+            pltpu.VMEM((QUADRANTS, per, cap + 2, SUB, RUN), jnp.float32),
+            pltpu.VMEM((QUADRANTS, per, SUB, points), jnp.float32),
+            pltpu.SemaphoreType.DMA((QUADRANTS,)),
+            pltpu.SemaphoreType.DMA((QUADRANTS,)),
+            pltpu.SemaphoreType.DMA((QUADRANTS,)),
+        ]
+        + ([pltpu.VMEM((SUB, points), jnp.float32)] if end else []),
         input_output_aliases=aliases,
         cost_estimate=pl.CostEstimate(flops=4 * cells, bytes_accessed=12 * cells, transcendentals=0),
         compiler_params=pltpu.CompilerParams(vmem_limit_bytes=VMEM_GRANT),
@@ -713,38 +759,42 @@
     total = deck.shape[0] // RUN
     row_runs = wet.shape[1] // RUN
     chunks = comps // (devices * SUB)
-    small = (runs * 25 + 31) // 32
+    small = (runs * 3 + 3) // 4
 
     deck = deck.reshape(total, RUN)
     wind = wind[None, :]
     limiter = limiter[None, :]
     growth = growth.reshape(comps // RUN, RUN)
     whitecap = whitecap.reshape(comps // RUN, RUN)
-    sent_small, sent_full, own_idxu, own_idxp, own_off, ratio, need = begin(
+    sent_small, sent_full, own_code, own_idxp, own_off, ratio, need = begin(
         small, runs, row_runs, devices, rank[None].astype(jnp.int32), deck, wet, wind, limiter,
         growth, whitecap, spectrum,
     )
 
     def branch(cap, first):
         def run(spectrum):
+            all_cross, all_along = courants(jnp.arange(comps, dtype=jnp.int32), courant)
+            decay = jnp.ones((comps,), jnp.float32)
+            for n in range(MAXSUB):
+                decay = jnp.where(n < substeps, decay * (1.0 - jnp.abs(all_cross) - jnp.abs(all_along)), decay)
+            decay = jnp.broadcast_to(decay[:, None], (comps, RUN))
             kept = []
             received = []
             for chunk in range(chunks):
                 held, *sent = sources(
                     cap, chunk, devices, chunk > 0, own_off, wind, limiter, ratio, growth, whitecap,
-                    own_idxp, spectrum,
+                    own_idxp, own_code, decay, spectrum,
                 )
                 kept.append(held)
-                sent = sent[0] if sent else first
+                sent = sent[0] if sent else first.reshape(devices, cap, SUB, RUN)
                 received.append(lax.all_to_all(sent, axes, split_axis=0, concat_axis=0, tiled=True))
-            idxu, idxp, off, slot = tables(runs, row_runs, deck, wet)
-            off, slot = off.reshape(total), slot.reshape(total)
             wet_runs = wet.reshape(total, RUN)
             returned = []
             for chunk in range(chunks):
-                mine = (chunk * devices + rank) * SUB + jnp.arange(SUB, dtype=jnp.int32)
-                cross, along = courants(mine, courant)
-                counts = substeps[mine]
+                begin_at = (chunk * devices + rank) * SUB
+                cross = lax.dynamic_slice_in_dim(all_cross, begin_at, SUB)
+                along = lax.dynamic_slice_in_dim(all_along, begin_at, SUB)
+                counts = lax.dynamic_slice_in_dim(substeps, begin_at, SUB)
                 info = jnp.stack(
                     [
                         jnp.where(cross[0] > 0, -row_runs, row_runs),
@@ -752,9 +802,12 @@
                         jnp.max(counts),
                     ]
                 ).astype(jnp.int32)
+                if chunk == 0:
+                    idxu, idxp, off_in, off_out, slot = tables(runs, row_runs, info, deck, wet)
+                    off_in, off_out, slot = (v.reshape(total) for v in (off_in, off_out, slot))
                 wide = lambda v: jnp.broadcast_to(v[:, None], (SUB, RUN))
                 sent = propagate(
-                    cap, runs, row_runs, slot, off, info, received[chunk].reshape(devices * cap, SUB, RUN),
+                    cap, runs, row_runs, slot, off_in, off_out, info, received[chunk].reshape(devices * cap, SUB, RUN),
                     idxu, idxp, wet_runs, wide(jnp.abs(cross)), wide(jnp.abs(along)), wide(counts),
                 )
                 returned.append(
@@ -765,10 +818,10 @@
             out, sums = None, None
             for chunk in range(chunks):
                 out, sums = finish(
-                    cap, comps, chunk, chunk == 0, chunk == chunks - 1, own_off, own_idxu,
+                    cap, comps, chunk, chunk == 0, chunk == chunks - 1, own_off, own_code,
                     returned[chunk], kept[chunk], sums, out,
                 )
-            return out, sums[0]
+            return out.reshape(comps, points), sums.reshape(points)
 
         return run
 
@@ -780,6 +833,8 @@
     runs = points // RUN
     return (
         comps % (devices * SUB) == 0
+        and comps > devices * SUB
+        and QUADRANTS * runs == RUN
         and devices % 16 == 0
         and runs % SUB == 0
         and RUN % runs == 0

time: 337 us -> 324 us (0.961)
  Pallas kernels: 120 us -> 109 us
  other arithmetic: 4.08 us -> 13.6 us
  waiting for transfers between devices: 182 us -> 173 us
    all_to_all x2, waiting for transfers between devices: 88.4 us -> 76.3 us  [run(): lax.all_to_all(sent, axes, split_axis=0, concat_axis=0, tiled=True)]
    pallas_call x5, Pallas kernels: 97.8 us -> 87.5 us  [the longest x2 60.4 us: propagate(): pl.pallas_call(body, in_specs=[smem] * 4 + [vmem] * 7, out_specs=vmem, ou...]
    select_n x2 -> x1, other arithmetic: 0.03 us -> 5.74 us  [run(): jnp.where(n < substeps, decay * (1.0 - jnp.abs(all_cross) - jnp.abs(all_a...]
    gather x2 -> x10, other arithmetic: 0.01 us -> 4.64 us  [courants(): speed = courant[comps // DIRS]]
  transfers between devices with their start and end apart: 4 -> 4, of which waited for: 4 -> 4; matrix products, arithmetic and copies ran while one was open for 3% -> 6% of each run, Pallas kernels for 31% -> 29%
where the time goes in v3:
time: 324 us; the launch traced here: 323 us
  waiting for transfers between devices  173 us (53%)
  Pallas kernels  109 us (34%)
  starting transfers between devices  19.6 us (6%)
  other arithmetic  13.6 us (4%)
  local copies, waits for them, and re-layouts  6.36 us (2%)
    all_to_all x2, waiting for transfers between devices, run(): lax.all_to_all(sent.reshape(devices, cap, SUB, RUN), axes, split_axis=0,...  96.4 us
    all_to_all x2, waiting for transfers between devices, run(): lax.all_to_all(sent, axes, split_axis=0, concat_axis=0, tiled=True)  76.3 us
    pallas_call x2, Pallas kernels, propagate(): pl.pallas_call(body, in_specs=[smem] * 4 + [vmem] * 7, out_specs=vmem, ou...  60.4 us
    pallas_call x2, Pallas kernels, finish(): pl.pallas_call(body, grid=(1,), in_specs=specs, out_specs=[far, whole(*la...  14.8 us
    pallas_call x2, Pallas kernels, sources(): pl.pallas_call(body, grid=(steps,), in_specs=[pl.BlockSpec(memory_space=p...  12.8 us
    pallas_call x1, Pallas kernels, tables(): pl.pallas_call(body, in_specs=[smem, vmem, vmem], out_specs=[vmem] * 5, o...  12.2 us
    all_to_all x2, starting transfers between devices, run(): lax.all_to_all(sent, axes, split_axis=0, concat_axis=0, tiled=True)  11.5 us
    pallas_call x1, Pallas kernels, begin(): pl.pallas_call(body, in_specs=[smem, vmem, vmem, vmem, vmem, vmem, vmem,...  8.69 us
  transfers between devices with their start and end apart: 4, of which 4 were waited for; matrix products, arithmetic and copies ran while one was open for 6% of the time, Pallas kernels for 29%

profile of v3, /device:TPU:0, one launch (start us, length us, event | category | flops | bytes accessed | tf_op | source)
XLA Modules:
  0.0 323.3 jit_solution(15389788205681864916)
XLA Ops:
  0.7 8.7 %begin.1 = (f32[8,4,24,8,128]{4,3,2,1,0:T(8,128)}, f32[8,4,32,8,128]{4,3,2,1,0:T(8,128)}, s32[128,128]{1,0:T(8,128)S(1)}, s32[128,128]{1,0:T(8,128)S(1)}, s32[12...) custom-call(s32[1]{0:T(128)} %bitcast.66.refs_0_, s32[1024,128]{1,0:T(8,128)} %bitcast.94, s32[256,512]{1,0:T(8,128)} %refs_2_.1, ...), custom_call_target="tpu_custom_call" | custom-call | flops 20971520 | bytes 20971520 | tf_op jit(solution)/shard_map/begin/pallas_call | solution.py:368
  10.1 313.0 %conditional.1 = ((f32[16,4,8,4096]{3,2,1,0:T(8,128)}, f32[32,128]{1,0:T(8,128)})) conditional(s32[]{:T(128)} %bitcast.72, (f32[16]{0:T(128)S(1)}, s32[]{:T(128)}, s32[512]{0:T(512)S(1)}, s32[1024,128]{1,0:T(8,128)S(1)}, s32[256,512]{1,0:T(8,128)S(1)}, /*index=5*/f32[512]{0:T(512)S(1)}, f32[512]{0:T(512)S(1)}, s32[128,128]{1,0:T(8,128)S(1)}, ...), branch_computations={%region_0.3_spmd, %region_3.6_spmd} | conditional | flops 776043072 | bytes 188010752 | solution.py:828
  10.4 7.4 %all-to-all-start.6 = ((f32[32,24,8,128]{3,2,1,0:T(8,128)}), f32[32,24,8,128]{3,2,1,0:T(8,128)}, u32[]{:S(2)}, u32[]{:S(2)}) async-start(f32[32,24,8,128]{3,2,1,0:T(8,128)} %bitcast.93), calls=%async_computation.6 | async-start | bytes 6291456 | tf_op jit(solution)/shard_map/cond/branch_1_fun/all_to_all | solution.py:790
  18.1 0.7 fusion.25
  18.8 4.3 %compare_select_fusion.8 = f32[512,1]{0,1:T(1,128)S(1)} fusion(f32[]{:T(128)} %bitcast.42, f32[]{:T(128)} %bitcast.43, f32[]{:T(128)} %bitcast.44, f32[]{:T(128)} %bitcast.45, f32[]{:T(128)} %bitcast.46, f32[]{:T(128)} %bitcast.48, f32[]{:T(128)} %bitcast.47), kind=kLoop, calls=%fused_computation.50 | loop fusion | flops 11776 | bytes 2076 | tf_op jit(solution)/shard_map/cond/branch_1_fun/gather | solution.py:99
  23.2 5.7 %multiply_select_fusion.7 = (f32[512]{0:T(512)S(1)}, f32[512]{0:T(512)S(1)}) fusion(s32[512]{0:T(512)S(1)} %get-tuple-element.90, pred[512]{0:T(512)(128)(4,1)S(1)} %compare_reduce_fusion.9, pred[512]{0:T(512)(128)(4,1)S(1)} %compare_reduce_fusion.10, pred[512]{0:T(512)(128)(4,1)S(1)} %compare_reduce_fusion.11, pred[512]{0:T(512)(128)(4,1)S(1)} %compare_reduce_fusion.12, ...), kind=kLoop, calls=%fused_computation.60 | loop fusion | flops 24064 | bytes 12836 | tf_op jit(solution)/shard_map/cond/branch_1_fun/jit(_where)/select_n | solution.py:779
  28.9 0.8 broadcast_in_dim.9.refs_8_
  29.8 7.3 %sources.6 = (f32[256,4096]{1,0:T(8,128)}, f32[32,24,8,128]{3,2,1,0:T(8,128)}) custom-call(s32[128,128]{1,0:T(8,128)S(1)} %get-tuple-element.86.refs_0_, f32[1,4096]{1,0:T(1,128)S(1)} %get-tuple-element.96.refs_1_, s32[1,4096]{1,0:T(1,128)S(1)} %get-tuple-element.97.refs_2_, f32[8,4096]{1,0:T(8,128)S(1)} %get-tuple-element.98.refs_3_, ...), custom_call_target="tpu_custom_call" | custom-call | flops 10485760 | bytes 12582912 | tf_op jit(solution)/shard_map/cond/branch_1_fun/sources/pallas_call | solution.py:492
  37.1 52.2 %all-to-all-done.6 = f32[32,24,8,128]{3,2,1,0:T(8,128)} async-done(((f32[32,24,8,128]{3,2,1,0:T(8,128)}), f32[32,24,8,128]{3,2,1,0:T(8,128)}, u32[]{:S(2)}, u32[]{:S(2)}) %all-to-all-start.6) | async-done | bytes 3145760 | tf_op jit(solution)/shard_map/cond/branch_1_fun/all_to_all | solution.py:790
  89.3 4.0 %all-to-all-start.4 = ((f32[32,24,8,128]{3,2,1,0:T(8,128)}), f32[32,24,8,128]{3,2,1,0:T(8,128)}, u32[]{:S(2)}, u32[]{:S(2)}) async-start(f32[32,24,8,128]{3,2,1,0:T(8,128)} %get-tuple-element.103), calls=%async_computation.4 | async-start | bytes 6291456 | tf_op jit(solution)/shard_map/cond/branch_1_fun/all_to_all | solution.py:790
  93.4 0.1 fusion.20
  93.5 0.8 reshape.241.refs_7_
  94.4 0.7 fusion.22
  95.1 1.2 pad_add_fusion.2.refs_0_.refs_3_
  96.3 12.2 %tables.3 = (s32[1024,128]{1,0:T(8,128)}, s32[1024,128]{1,0:T(8,128)}, s32[8,128]{1,0:T(8,128)}, s32[8,128]{1,0:T(8,128)}, s32[8,128]{1,0:T(8,128)}) custom-call(s32[3]{0:T(128)} %pad_add_fusion.2.refs_0_.refs_3_, s32[1024,128]{1,0:T(8,128)S(1)} %get-tuple-element.91.refs_1_, s32[256,512]{1,0:T(8,128)S(1)} %get-tuple-element.92.refs_2_), custom_call_target="tpu_custom_call" | custom-call | flops 536870912 | bytes 2097152 | tf_op jit(solution)/shard_map/cond/branch_1_fun/tables/pallas_call | solution.py:435
  108.5 0.7 broadcast_in_dim.22.refs_10_
  109.1 0.7 broadcast_in_dim.21.refs_9_
  109.8 0.7 broadcast_in_dim.20.refs_8_
  110.5 30.2 %propagate.7 = f32[768,8,128]{2,1,0:T(8,128)} custom-call(s32[1024]{0:T(1024)} %bitcast.123, s32[1024]{0:T(1024)} %bitcast.119, s32[1024]{0:T(1024)} %bitcast.121, s32[3]{0:T(128)} %pad_add_fusion.2.refs_0_.refs_3_, f32[768,8,128]{2,1,0:T(8,128)} %bitcast.62.refs_4_, s32[1024,128]{1,0:T(8,128)} %get-tuple-element.104.refs_5_, ...), custom_call_target="tpu_custom_call" | custom-call | flops 104857600 | bytes 41943040 | tf_op jit(solution)/shard_map/cond/branch_1_fun/propagate/pallas_call | solution.py:634
  140.6 24.1 %all-to-all-done.4 = f32[32,24,8,128]{3,2,1,0:T(8,128)} async-done(((f32[32,24,8,128]{3,2,1,0:T(8,128)}), f32[32,24,8,128]{3,2,1,0:T(8,128)}, u32[]{:S(2)}, u32[]{:S(2)}) %all-to-all-start.4) | async-done | bytes 3145760 | tf_op jit(solution)/shard_map/cond/branch_1_fun/all_to_all | solution.py:790
  164.8 4.0 %all-to-all-start.7 = ((f32[32,24,8,128]{3,2,1,0:T(8,128)}), f32[32,24,8,128]{3,2,1,0:T(8,128)}, u32[]{:S(2)}, u32[]{:S(2)}) async-start(f32[32,24,8,128]{3,2,1,0:T(8,128)} %bitcast.88), calls=%async_computation.7 | async-start | bytes 6291456 | tf_op jit(solution)/shard_map/cond/branch_1_fun/all_to_all | solution.py:814
  168.9 1.2 pad_add_fusion.3.refs_3_
  170.1 0.7 broadcast_in_dim.19.refs_10_
  170.7 0.7 broadcast_in_dim.18.refs_9_
  171.4 0.7 broadcast_in_dim.17.refs_8_
  172.1 30.3 %propagate.6 = f32[768,8,128]{2,1,0:T(8,128)} custom-call(s32[1024]{0:T(1024)} %bitcast.124, s32[1024]{0:T(1024)} %bitcast.120, s32[1024]{0:T(1024)} %bitcast.122, s32[3]{0:T(128)} %pad_add_fusion.3.refs_3_, f32[768,8,128]{2,1,0:T(8,128)} %bitcast.57.refs_4_, s32[1024,128]{1,0:T(8,128)} %get-tuple-element.104.refs_5_, ...), custom_call_target="tpu_custom_call" | custom-call | flops 104857600 | bytes 41943040 | tf_op jit(solution)/shard_map/cond/branch_1_fun/propagate/pallas_call | solution.py:634
  202.3 37.9 %all-to-all-done.7 = f32[32,24,8,128]{3,2,1,0:T(8,128)} async-done(((f32[32,24,8,128]{3,2,1,0:T(8,128)}), f32[32,24,8,128]{3,2,1,0:T(8,128)}, u32[]{:S(2)}, u32[]{:S(2)}) %all-to-all-start.7) | async-done | bytes 3145760 | tf_op jit(solution)/shard_map/cond/branch_1_fun/all_to_all | solution.py:814
  240.3 4.0 %all-to-all-start.5 = ((f32[32,24,8,128]{3,2,1,0:T(8,128)}), f32[32,24,8,128]{3,2,1,0:T(8,128)}, u32[]{:S(2)}, u32[]{:S(2)}) async-start(f32[32,24,8,128]{3,2,1,0:T(8,128)} %bitcast.89), calls=%async_computation.5 | async-start | bytes 6291456 | tf_op jit(solution)/shard_map/cond/branch_1_fun/all_to_all | solution.py:814
  244.3 5.5 %sources.7 = f32[256,4096]{1,0:T(8,128)} custom-call(s32[128,128]{1,0:T(8,128)S(1)} %get-tuple-element.86.refs_0_, f32[1,4096]{1,0:T(1,128)S(1)} %get-tuple-element.96.refs_1_, s32[1,4096]{1,0:T(1,128)S(1)} %get-tuple-element.97.refs_2_, f32[8,4096]{1,0:T(8,128)S(1)} %get-tuple-element.98.refs_3_, f32[4,1,128]{2,1,0:T(1,128)S(1)} %bitcast.107, ...), custom_call_target="tpu_custom_call" | custom-call | flops 10485760 | bytes 12582912 | tf_op jit(solution)/shard_map/cond/branch_1_fun/sources/pallas_call | solution.py:492
  249.8 7.4 %finish.6 = (f32[16,4,8,4096]{3,2,1,0:T(8,128)}, f32[8,4096]{1,0:T(8,128)}) custom-call(s32[128,128]{1,0:T(8,128)S(1)} %get-tuple-element.86.refs_0_, s32[128,128]{1,0:T(8,128)S(1)} %get-tuple-element.87.refs_7_.refs_1_, f32[8,4,24,8,128]{4,3,2,1,0:T(8,128)} %bitcast.64.refs_2_, f32[8,4,8,4096]{3,2,1,0:T(8,128)} %bitcast.84), custom_call_target="tpu_custom_call" | custom-call | flops 4194304 | bytes 12582912 | tf_op jit(solution)/shard_map/cond/branch_1_fun/finish/pallas_call | solution.py:728
  257.3 58.5 %all-to-all-done.5 = f32[32,24,8,128]{3,2,1,0:T(8,128)} async-done(((f32[32,24,8,128]{3,2,1,0:T(8,128)}), f32[32,24,8,128]{3,2,1,0:T(8,128)}, u32[]{:S(2)}, u32[]{:S(2)}) %all-to-all-start.5) | async-done | bytes 3145760 | tf_op jit(solution)/shard_map/cond/branch_1_fun/all_to_all | solution.py:814
  315.8 7.4 %finish.7 = (f32[16,4,8,4096]{3,2,1,0:T(8,128)}, f32[32,128]{1,0:T(8,128)}) custom-call(s32[128,128]{1,0:T(8,128)S(1)} %get-tuple-element.86.refs_0_, s32[128,128]{1,0:T(8,128)S(1)} %get-tuple-element.87.refs_7_.refs_1_, f32[8,4,24,8,128]{4,3,2,1,0:T(8,128)} %bitcast.59.refs_2_, f32[8,4,8,4096]{3,2,1,0:T(8,128)} %bitcast.92, ...), custom_call_target="tpu_custom_call", output_to_operand_aliasing={{0}: (5, {})} | custom-call | flops 4194304 | bytes 12582912 | tf_op jit(solution)/shard_map/cond/branch_1_fun/finish/pallas_call | solution.py:728
  (26 shorter events, 0.4 us)
Async XLA Ops:
  0.6 9.4 %copy-start = (s32[256,512]{1,0:T(8,128)S(1)}, s32[256,512]{1,0:T(8,128)}, u32[]{:S(2)}) copy-start(s32[256,512]{1,0:T(8,128)} %refs_2_.1) | copy-start | bytes 1572868
  0.6 9.4 %copy-start.1 = (s32[131072]{0:T(1024)S(1)}, s32[131072]{0:T(1024)}, u32[]{:S(2)}) copy-start(s32[131072]{0:T(1024)} %param.18) | copy-start | bytes 1572868
  0.7 9.4 %copy-start.2 = (f32[16]{0:T(128)S(1)}, f32[16]{0:T(128)}, u32[]{:S(2)}) copy-start(f32[16]{0:T(128)} %param.15) | copy-start | bytes 196
  0.7 9.4 %copy-start.3 = (f32[4096]{0:T(1024)S(1)}, f32[4096]{0:T(1024)}, u32[]{:S(2)}) copy-start(f32[4096]{0:T(1024)} %param.12) | copy-start | bytes 49156
  0.7 9.4 %copy-start.4 = (s32[4096]{0:T(1024)S(1)}, s32[4096]{0:T(1024)}, u32[]{:S(2)}) copy-start(s32[4096]{0:T(1024)} %param.17) | copy-start | bytes 49156
  0.7 9.4 %copy-start.5 = (f32[512]{0:T(512)S(1)}, f32[512]{0:T(512)}, u32[]{:S(2)}) copy-start(f32[512]{0:T(512)} %param.13) | copy-start | bytes 6148
  0.7 9.4 %copy-start.6 = (f32[512]{0:T(512)S(1)}, f32[512]{0:T(512)}, u32[]{:S(2)}) copy-start(f32[512]{0:T(512)} %param.14) | copy-start | bytes 6148
  0.7 9.4 %copy-start.7 = (s32[512]{0:T(512)S(1)}, s32[512]{0:T(512)}, u32[]{:S(2)}) copy-start(s32[512]{0:T(512)} %param.16) | copy-start | bytes 6148
  10.4 78.9 %all-to-all-start.6 = ((f32[32,24,8,128]{3,2,1,0:T(8,128)}), f32[32,24,8,128]{3,2,1,0:T(8,128)}, u32[]{:S(2)}, u32[]{:S(2)}) async-start(f32[32,24,8,128]{3,2,1,0:T(8,128)} %bitcast.93), calls=%async_computation.6 | async-start | bytes 6291456 | tf_op jit(solution)/shard_map/cond/branch_1_fun/all_to_all | solution.py:790
  89.3 75.5 %all-to-all-start.4 = ((f32[32,24,8,128]{3,2,1,0:T(8,128)}), f32[32,24,8,128]{3,2,1,0:T(8,128)}, u32[]{:S(2)}, u32[]{:S(2)}) async-start(f32[32,24,8,128]{3,2,1,0:T(8,128)} %get-tuple-element.103), calls=%async_computation.4 | async-start | bytes 6291456 | tf_op jit(solution)/shard_map/cond/branch_1_fun/all_to_all | solution.py:790
  164.8 75.5 %all-to-all-start.7 = ((f32[32,24,8,128]{3,2,1,0:T(8,128)}), f32[32,24,8,128]{3,2,1,0:T(8,128)}, u32[]{:S(2)}, u32[]{:S(2)}) async-start(f32[32,24,8,128]{3,2,1,0:T(8,128)} %bitcast.88), calls=%async_computation.7 | async-start | bytes 6291456 | tf_op jit(solution)/shard_map/cond/branch_1_fun/all_to_all | solution.py:814
  240.3 75.5 %all-to-all-start.5 = ((f32[32,24,8,128]{3,2,1,0:T(8,128)}), f32[32,24,8,128]{3,2,1,0:T(8,128)}, u32[]{:S(2)}, u32[]{:S(2)}) async-start(f32[32,24,8,128]{3,2,1,0:T(8,128)} %bitcast.89), calls=%async_computation.5 | async-start | bytes 6291456 | tf_op jit(solution)/shard_map/cond/branch_1_fun/all_to_all | solution.py:814
